TPU v7x, 128 devices: a whole 4x4x4 slice. The times are simulated.
128 devices in a mesh: grp: 4 (over x), dev: 32 (over z, y, core).
Axes of the slice: x: 4, y: 4, z: 4, core: 2. Of those that a mesh axis runs over, the one named last changes fastest.
Arguments:
- tokens: bfloat16 [131072, 3584], P(('grp', 'dev')), may hold values from -160 to 160
- input_norm_gain: bfloat16 [3584], replicated, may hold values from 0.5 to 1.5
- base_query_value_weight: bfloat16 [3584, 2304], P('grp'), may hold values from -0.09375 to 0.09375
- adapter_down_weight: bfloat16 [128, 3584, 128], P('dev'), may hold values from -0.09375 to 0.09375
- adapter_up_query: bfloat16 [128, 64, 1792], P('dev'), may hold values from -0.75 to 0.75
- adapter_up_value: bfloat16 [128, 64, 512], P('dev'), may hold values from -0.75 to 0.75
- token_adapter_id: int32 [131072, 1], P(('grp', 'dev')), may hold values from 0 to 127, as said below
- adapter_storage_row: int32 [128], replicated, may hold values from 0 to 127, as said below
Outputs:
- adapted_query_output: bfloat16 [131072, 1792], P(('grp', 'dev'))
- adapted_value_output: bfloat16 [131072, 512], P(('grp', 'dev'))
Inputs may be any that keep to these rules, and one draw needn't show every extreme that they name: `token_adapter_id`: no adapter is named by more than 16 of the rows of one device, and in every device's rows one adapter is named exactly 16 times. Adapters whose storage rows lie on one index of dev (rows k * 4 to k * 4 + 3) are named by at most 48 of the rows of one device, and exactly 48 times for some index in every device's rows. A permutation: the adapter with id a is row adapter_storage_row[a] of adapter_down_weight, adapter_up_query and adapter_up_value.
All inputs are finite; a program needn't handle non-finite values.
Results may differ from a plain program's by a relative error of at most 0.0054.
Values may be sent and summed in bfloat16 or wider, within the bound.
No kernel may reach another device: no remote copies, remote signals or barrier semaphores. Data moves between devices by JAX's collectives and lax.ppermute only.
A program may use at most 256 MiB of HBM per device.

v0:
```python
import jax
import jax.numpy as jnp
from jax import lax
from jax.sharding import PartitionSpec as P

adapter_scale = 0.5


def for_sending(shard):

    def short(part):
        return part.astype(jnp.bfloat16) if part.dtype == jnp.float32 else part

    return jax.tree.map(short, shard)


def normalize(tokens, input_norm_gain):
    values = tokens.astype(jnp.float32)
    factor = lax.rsqrt(jnp.mean(values * values, axis=1, keepdims=True) + 1e-06)
    return (values * factor * input_norm_gain.astype(jnp.float32)[None, :]).astype(jnp.bfloat16)


def project_downward(incoming_rows, adapter_down_weight):
    return jnp.einsum(
        "jepo,eon->jepn", incoming_rows, adapter_down_weight, preferred_element_type=jnp.float32
    ).astype(jnp.bfloat16)


def project_upward(reduced_rank_state, adapter_up_query, adapter_up_value, rank_halves):
    delta_q = jnp.einsum(
        "gjxm,jmt->gjxt",
        reduced_rank_state[..., :rank_halves],
        adapter_up_query,
        preferred_element_type=jnp.float32,
    ).astype(jnp.bfloat16)
    delta_v = jnp.einsum(
        "gjxm,jmt->gjxt",
        reduced_rank_state[..., rank_halves:],
        adapter_up_value,
        preferred_element_type=jnp.float32,
    ).astype(jnp.bfloat16)
    return (delta_q, delta_v)


def body(
    tokens,
    input_norm_gain,
    base_query_value_weight,
    adapter_down_weight,
    adapter_up_query,
    adapter_up_value,
    token_adapter_id,
    adapter_storage_row,
):
    tok_rows = tokens.shape[0]
    feature_count = tokens.shape[1]
    adapter_local_rows = adapter_down_weight.shape[0]
    rank_couple = adapter_down_weight.shape[2]
    rank_halves = rank_couple // 2
    query_column_range = adapter_up_query.shape[2]
    value_column_range = adapter_up_value.shape[2]
    dev_count = lax.axis_size("dev")
    pool_size = adapter_local_rows * dev_count
    capacity = 2 * tok_rows // pool_size
    normed = normalize(tokens, input_norm_gain)
    catalog = jnp.arange(pool_size, dtype=jnp.int32)
    choose = token_adapter_id == catalog[None, :]
    slot_of = jnp.sum(jnp.where(choose, adapter_storage_row[None, :], 0), axis=1)
    onehot = (slot_of[:, None] == catalog[None, :]).astype(jnp.int32)
    before = jnp.cumsum(onehot, axis=0) - onehot
    position = jnp.sum(onehot * before, axis=1)
    target = slot_of * capacity + position
    sending_rows = (
        jnp.zeros((pool_size * capacity, feature_count), jnp.bfloat16).at[target].set(normed)
    )
    sending_rows = sending_rows.reshape(dev_count, adapter_local_rows, capacity, feature_count)
    reduced_rank_state = project_downward(
        lax.all_to_all(sending_rows, "dev", split_axis=0, concat_axis=0, tiled=True),
        adapter_down_weight,
    )
    answer = lax.all_to_all(
        for_sending(
            project_upward(reduced_rank_state, adapter_up_query, adapter_up_value, rank_halves)
        ),
        "dev",
        split_axis=0,
        concat_axis=0,
        tiled=True,
    )
    base_product = jnp.dot(
        normed,
        lax.all_gather(base_query_value_weight, "grp", axis=0, tiled=True),
        preferred_element_type=jnp.float32,
    )
    delta_q, delta_v = answer
    query_rank_rows = delta_q.reshape(pool_size * capacity, query_column_range)[target]
    value_rank_rows = delta_v.reshape(pool_size * capacity, value_column_range)[target]
    adapted_query_output = (
        base_product[:, :query_column_range] + adapter_scale * query_rank_rows.astype(jnp.float32)
    ).astype(jnp.bfloat16)
    adapted_value_output = (
        base_product[:, query_column_range:] + adapter_scale * value_rank_rows.astype(jnp.float32)
    ).astype(jnp.bfloat16)
    return (adapted_query_output, adapted_value_output)


def solution(mesh):
    in_specs = (
        P(("grp", "dev"), None),
        P(),
        P("grp", None),
        P("dev", None, None),
        P("dev", None, None),
        P("dev", None, None),
        P(("grp", "dev"), None),
        P(),
    )
    out_specs = (P(("grp", "dev"), None), P(("grp", "dev"), None))
    return jax.shard_map(body, mesh=mesh, in_specs=in_specs, out_specs=out_specs, check_vma=False)
```

profile of v0, /device:TPU:0, one launch (start us, length us, event | category | flops | bytes accessed | tf_op | source)
XLA Modules:
  0.0 425.0 jit_solution(15376310033949170737)
XLA Ops:
  7.2 1.1 select_reduce_fusion
  8.9 0.4 fusion.24
  9.2 0.9 convert_element_type.47
  10.2 4.9 %fusion = f32[1024]{0:T(1024)S(1)} fusion(bf16[1024,3584]{1,0:T(8,128)(2,1)} %param.8), kind=kLoop, calls=%fused_computation.5 | loop fusion | flops 11009024 | bytes 7344128 | tf_op jit(solution)/shard_map/reduce_sum | solution.py:19
  15.1 6.1 %fusion.2 = bf16[1024,3584]{1,0:T(8,128)(2,1)} fusion(bf16[1024,3584]{1,0:T(8,128)(2,1)S(1)} %copy-done.2, f32[3584]{0:T(1024)S(1)} %convert_element_type.47, f32[1024]{0:T(1024)S(1)} %add_rsqrt_fusion), kind=kLoop, calls=%fused_computation.7 | loop fusion | flops 14680064 | bytes 14698496 | tf_op jit(solution)/shard_map/convert_element_type | solution.py:20
  21.2 19.7 %scatter_custom_fusion = bf16[2048,3584]{1,0:T(8,128)(2,1)} fusion(s32[1024]{0:T(1024)S(1)} %bitcast.48, bf16[1024,3584]{1,0:T(8,128)(2,1)} %fusion.2, bf16[]{:T(256)} %constant.4.clone.1), kind=kCustom, calls=%fused_computation.13 | custom fusion | bytes 14680576 | tf_op jit(solution)/shard_map/scatter | solution.py:74
  40.9 8.5 %all-to-all-start = ((bf16[32,4,16,3584]{3,2,1,0:T(8,128)(2,1)}), bf16[32,4,16,3584]{3,2,1,0:T(8,128)(2,1)}, u32[]{:S(2)}, u32[]{:S(2)}) async-start(bf16[32,4,16,3584]{3,2,1,0:T(8,128)(2,1)} %bitcast.44), calls=%async_computation | async-start | bytes 29360128 | tf_op jit(solution)/shard_map/all_to_all | solution.py:78
  49.5 0.3 all-gather.2.cloned.1.call-start
  49.7 0.5 all-gather.2.cloned.1.call-update
  50.2 185.8 %all-to-all-done = bf16[32,4,16,3584]{3,2,1,0:T(8,128)(2,1)} async-done(((bf16[32,4,16,3584]{3,2,1,0:T(8,128)(2,1)}), bf16[32,4,16,3584]{3,2,1,0:T(8,128)(2,1)}, u32[]{:S(2)}, u32[]{:S(2)}) %all-to-all-start) | async-done | bytes 14680096 | tf_op jit(solution)/shard_map/all_to_all | solution.py:78
  236.0 10.2 %fusion.15 = bf16[32,4,16,128]{3,2,0,1:T(8,128)(2,1)S(1)} fusion(bf16[4,3584,128]{2,1,0:T(8,128)(2,1)} %param.11, bf16[32,4,16,3584]{3,2,1,0:T(8,128)(2,1)} %all-to-all-done), kind=kOutput, calls=%fused_computation.20 | convolution fusion | flops 1879310336 | bytes 18874368 | tf_op jit(solution)/shard_map/jepo,eon->jepn/dot_general | solution.py:24
  246.2 0.7 convert_bitcast_fusion.1
  247.0 1.5 copy.19
  248.5 4.0 all-to-all-start.2
  252.5 2.0 convert_bitcast_fusion
  254.6 4.0 copy.18
  258.6 23.9 %all-to-all-done.2 = bf16[32,4,16,512]{3,2,1,0:T(8,128)(2,1)S(1)} async-done(((bf16[32,4,16,512]{3,2,1,0:T(8,128)(2,1)}), bf16[32,4,16,512]{3,2,1,0:T(8,128)(2,1)S(1)}, u32[]{:S(2)}, u32[]{:S(2)}) %all-to-all-start.2) | async-done | bytes 2097184 | tf_op jit(solution)/shard_map/all_to_all | solution.py:81
  282.5 5.2 %all-to-all-start.1 = ((bf16[32,4,16,1792]{3,2,1,0:T(8,128)(2,1)}), bf16[32,4,16,1792]{3,2,1,0:T(8,128)(2,1)}, u32[]{:S(2)}, u32[]{:S(2)}) async-start(bf16[32,4,16,1792]{3,2,1,0:T(8,128)(2,1)} %copy.18), calls=%async_computation.1 | async-start | bytes 14680064 | tf_op jit(solution)/shard_map/all_to_all | solution.py:81
  287.7 5.1 %gather_fusion.1 = bf16[1024,512]{1,0:T(8,128)(2,1)} fusion(bf16[2048,512]{1,0:T(8,128)(2,1)S(1)} %bitcast.45, s32[1024]{0:T(1024)S(1)} %broadcast_clamp_fusion), kind=kCustom, calls=%fused_computation.1 | custom fusion | bytes 2101248 | tf_op jit(solution)/shard_map/gather | solution.py:97
  292.8 86.9 %all-to-all-done.1 = bf16[32,4,16,1792]{3,2,1,0:T(8,128)(2,1)} async-done(((bf16[32,4,16,1792]{3,2,1,0:T(8,128)(2,1)}), bf16[32,4,16,1792]{3,2,1,0:T(8,128)(2,1)}, u32[]{:S(2)}, u32[]{:S(2)}) %all-to-all-start.1) | async-done | bytes 7340064 | tf_op jit(solution)/shard_map/all_to_all | solution.py:81
  379.7 12.0 %gather_fusion = bf16[1024,1792]{1,0:T(8,128)(2,1)} fusion(bf16[2048,1792]{1,0:T(8,128)(2,1)} %bitcast.14, s32[1024]{0:T(1024)S(1)} %broadcast_clamp_fusion), kind=kCustom, calls=%fused_computation | custom fusion | bytes 7344128 | tf_op jit(solution)/shard_map/gather | solution.py:96
  391.7 22.4 %fusion.29 = f32[1024,2304]{1,0:T(8,128)S(1)} fusion(bf16[1024,3584]{1,0:T(8,128)(2,1)} %fusion.2, bf16[3584,2304]{1,0:T(8,128)(2,1)} %all-gather.2.cloned.1.call-done), kind=kOutput, calls=%fused_computation.41 | convolution fusion | flops 16911433728 | bytes 33292288 | tf_op jit(solution)/shard_map/dot_general | solution.py:90
  414.1 2.8 fusion.5
  416.9 1.2 fusion.9
  (24 shorter events, 0.5 us)
Async XLA Ops:
  7.2 245.3 %copy-start = (bf16[4,64,1792]{2,1,0:T(8,128)(2,1)S(1)}, bf16[4,64,1792]{2,1,0:T(8,128)(2,1)}, u32[]{:S(2)}) copy-start(bf16[4,64,1792]{2,1,0:T(8,128)(2,1)} %param.12) | copy-start | bytes 2752516
  8.7 6.4 %copy-start.2 = (bf16[1024,3584]{1,0:T(8,128)(2,1)S(1)}, bf16[1024,3584]{1,0:T(8,128)(2,1)}, u32[]{:S(2)}) copy-start(bf16[1024,3584]{1,0:T(8,128)(2,1)} %param.8) | copy-start | bytes 22020100
  40.9 195.1 %all-to-all-start = ((bf16[32,4,16,3584]{3,2,1,0:T(8,128)(2,1)}), bf16[32,4,16,3584]{3,2,1,0:T(8,128)(2,1)}, u32[]{:S(2)}, u32[]{:S(2)}) async-start(bf16[32,4,16,3584]{3,2,1,0:T(8,128)(2,1)} %bitcast.44), calls=%async_computation | async-start | bytes 29360128 | tf_op jit(solution)/shard_map/all_to_all | solution.py:78
  49.5 342.2 %all-gather.2.cloned.1.call-start = ((), (), s32[]{:S(2)}) async-start(), calls=%async_computation.3 | async-start | bytes 20643840 | tf_op jit(solution)/shard_map/all_gather | solution.py:92
  50.2 196.0 %copy-start.5 = (bf16[4,64,512]{2,1,0:T(8,128)(2,1)S(1)}, bf16[4,64,512]{2,1,0:T(8,128)(2,1)}, u32[]{:S(2)}) copy-start(bf16[4,64,512]{2,1,0:T(8,128)(2,1)} %param.13) | copy-start | bytes 786436
  248.5 34.0 %all-to-all-start.2 = ((bf16[32,4,16,512]{3,2,1,0:T(8,128)(2,1)}), bf16[32,4,16,512]{3,2,1,0:T(8,128)(2,1)S(1)}, u32[]{:S(2)}, u32[]{:S(2)}) async-start(bf16[32,4,16,512]{3,2,1,0:T(8,128)(2,1)} %copy.19), calls=%async_computation.2 | async-start | bytes 4194304 | tf_op jit(solution)/shard_map/all_to_all | solution.py:81
  282.5 97.2 %all-to-all-start.1 = ((bf16[32,4,16,1792]{3,2,1,0:T(8,128)(2,1)}), bf16[32,4,16,1792]{3,2,1,0:T(8,128)(2,1)}, u32[]{:S(2)}, u32[]{:S(2)}) async-start(bf16[32,4,16,1792]{3,2,1,0:T(8,128)(2,1)} %copy.18), calls=%async_computation.1 | async-start | bytes 14680064 | tf_op jit(solution)/shard_map/all_to_all | solution.py:81
  391.7 22.4 %copy-start.3 = (bf16[1024,1792]{1,0:T(8,128)(2,1)S(1)}, bf16[1024,1792]{1,0:T(8,128)(2,1)}, u32[]{:S(2)}) copy-start(bf16[1024,1792]{1,0:T(8,128)(2,1)} %gather_fusion) | copy-start | bytes 11010052
  391.7 26.5 %copy-start.1 = (bf16[4,64,1792]{2,1,0:T(8,128)(2,1)S(1)}, bf16[4,64,1792]{2,1,0:T(8,128)(2,1)}, u32[]{:S(2)}) copy-start(bf16[4,64,1792]{2,1,0:T(8,128)(2,1)} %param.12) | copy-start | bytes 2752516
  414.1 2.8 copy-start.4
Sparse Core Ops, SparseCore 0:
  52.0 153.2 all-gather.1
where the time goes:
time: 425 us
  waiting for transfers between devices  297 us (70%)
  local copies, waits for them, and re-layouts  42.5 us (10%)
  matrix products  35.4 us (8%)
  starting transfers between devices  18 us (4%)
  other arithmetic  17.7 us (4%)
  between operations  14.2 us (3%)
    all_to_all x1, waiting for transfers between devices, body(): lax.all_to_all(sending_rows, 'dev', split_axis=0, concat_axis=0, tiled=True)  186 us
    all_to_all x2, waiting for transfers between devices, body(): lax.all_to_all(for_sending(project_upward(reduced_rank_state, adapter_up_...  111 us
    dot_general x1, matrix products, body(): jnp.dot(normed, lax.all_gather(base_query_value_weight, 'grp', axis=0, ti...  22.4 us
    scatter x1, local copies, waits for them, and re-layouts, body(): jnp.zeros((pool_size * capacity, feature_count), jnp.bfloat16).at[target]  19.7 us
    gather x1, local copies, waits for them, and re-layouts, body(): delta_q.reshape(pool_size * capacity, query_column_range)[target]  12 us
    dot_general x1, matrix products, project_downward(): jnp.einsum('jepo,eon->jepn', incoming_rows, adapter_down_weight, preferre...  10.2 us
    all_to_all x2, starting transfers between devices, body(): lax.all_to_all(for_sending(project_upward(reduced_rank_state, adapter_up_...  9.2 us
    all_to_all x1, starting transfers between devices, body(): lax.all_to_all(sending_rows, 'dev', split_axis=0, concat_axis=0, tiled=True)  8.53 us
  transfers between devices with their start and end apart: 4, of which 3 were waited for; matrix products, arithmetic and copies ran while one was open for 8% of the time, Pallas kernels for 0%

commit v1 on v0

v1 whole, which is shorter than its diff:
```python
import functools
import jax
import jax.numpy as jnp
from jax import lax
from jax.experimental import pallas as pl
from jax.experimental.pallas import tpu as pltpu
from jax.sharding import PartitionSpec as P

ADAPTER_SCALE = 0.5
DEVICE_CAP = 48
LINE = 4
BLOCK = LINE * DEVICE_CAP
BLOCKS = 2 * LINE
MIB = 1 << 20


def plan_kernel(coord_ref, ids_ref, row_ref, target_ref, count_ref):
    z, y, c = coord_ref[0], coord_ref[1], coord_ref[2]
    pool, toks = row_ref.shape[0], ids_ref.shape[1]
    catalog = lax.broadcasted_iota(jnp.int32, (pool, toks), 0)
    slot = jnp.sum(jnp.where(ids_ref[...] == catalog, row_ref[...], 0), axis=0, keepdims=True)
    chosen = (slot == catalog).astype(jnp.float32)
    chosen16 = chosen.astype(jnp.bfloat16)
    earlier = (
        lax.broadcasted_iota(jnp.int32, (toks, toks), 0) < lax.broadcasted_iota(jnp.int32, (toks, toks), 1)
    ).astype(jnp.float32).astype(jnp.bfloat16)
    before = jnp.dot(chosen16, earlier, preferred_element_type=jnp.float32)
    si = lax.broadcasted_iota(jnp.int32, (pool, pool), 0)
    sj = lax.broadcasted_iota(jnp.int32, (pool, pool), 1)
    lower = jnp.logical_and(lax.shift_right_logical(si, 2) == lax.shift_right_logical(sj, 2), sj < si)
    lower = lower.astype(jnp.float32).astype(jnp.bfloat16)
    offset = jnp.sum(jnp.dot(lower, chosen16, preferred_element_type=jnp.float32), axis=1, keepdims=True)
    rank = jnp.sum(chosen * (before + offset), axis=0, keepdims=True).astype(jnp.int32)
    owner = lax.shift_right_logical(slot, 2)
    owner_z = lax.shift_right_logical(owner, 3)
    owner_y = jnp.bitwise_and(lax.shift_right_logical(owner, 1), 3)
    owner_c = jnp.bitwise_and(owner, 1)
    dz = jnp.bitwise_and(owner_z - z + LINE, 3)
    dy = jnp.bitwise_and(owner_y - y + LINE, 3)
    step = jnp.where(owner_c == 0, dz, dy)
    sub = jnp.where(owner_c == 0, dy, dz)
    cross = jnp.bitwise_xor(owner_c, c)
    target_ref[...] = (cross * LINE + step) * BLOCK + sub * DEVICE_CAP + rank
    count_ref[...] = jnp.sum(chosen, axis=1, keepdims=True)


def plan(coords, ids, row):
    toks, pool = ids.shape[1], row.shape[0]
    return pl.pallas_call(
        plan_kernel,
        out_shape=(
            jax.ShapeDtypeStruct((1, toks), jnp.int32),
            jax.ShapeDtypeStruct((pool, 1), jnp.float32),
        ),
        in_specs=[
            pl.BlockSpec(memory_space=pltpu.SMEM),
            pl.BlockSpec(memory_space=pltpu.VMEM),
            pl.BlockSpec(memory_space=pltpu.VMEM),
        ],
        out_specs=(pl.BlockSpec(memory_space=pltpu.VMEM), pl.BlockSpec(memory_space=pltpu.VMEM)),
        compiler_params=pltpu.CompilerParams(vmem_limit_bytes=32 * MIB),
        name="plan",
    )(coords, ids, row)


def dispatch_kernel(target_ref, tokens_ref, gain_ref, normed_ref, *rest):
    blocks, (pick, factor) = rest[:BLOCKS], rest[BLOCKS:]
    k = pl.program_id(0)
    toks, feats = tokens_ref.shape
    chunk = normed_ref.shape[1]

    @pl.when(k == 0)
    def _():
        for b in range(BLOCKS):
            rows = lax.broadcasted_iota(jnp.int32, (BLOCK, toks), 0) + b * BLOCK
            pick[b] = (rows == target_ref[...]).astype(jnp.float32).astype(jnp.bfloat16)

        def sums(i, carry):
            part = tokens_ref[pl.ds(pl.multiple_of(i * 128, 128), 128), :].astype(jnp.float32)
            mean = jnp.sum(part * part, axis=1, keepdims=True) / feats
            factor[pl.ds(pl.multiple_of(i * 128, 128), 128), :] = lax.rsqrt(mean + 1e-06)
            return carry

        lax.fori_loop(0, toks // 128, sums, 0)

    cols = pl.ds(pl.multiple_of(k * chunk, 128), chunk)
    values = tokens_ref[:, cols].astype(jnp.float32)
    gain = gain_ref[:, cols].astype(jnp.float32)
    normed = (values * factor[...] * gain).astype(jnp.bfloat16)
    normed_ref[...] = normed
    for b in range(BLOCKS):
        blocks[b][...] = jnp.dot(pick[b], normed, preferred_element_type=jnp.float32).astype(jnp.bfloat16)


def dispatch(target, tokens, gain):
    toks, feats = tokens.shape
    chunk = 512
    return pl.pallas_call(
        dispatch_kernel,
        grid=(feats // chunk,),
        out_shape=(jax.ShapeDtypeStruct((toks, feats), jnp.bfloat16),)
        + (jax.ShapeDtypeStruct((BLOCK, feats), jnp.bfloat16),) * BLOCKS,
        in_specs=[
            pl.BlockSpec((1, toks), lambda k: (0, 0)),
            pl.BlockSpec((toks, feats), lambda k: (0, 0)),
            pl.BlockSpec((1, feats), lambda k: (0, 0)),
        ],
        out_specs=(pl.BlockSpec((toks, chunk), lambda k: (0, k)),)
        + (pl.BlockSpec((BLOCK, chunk), lambda k: (0, k)),) * BLOCKS,
        scratch_shapes=[
            pltpu.VMEM((BLOCKS, BLOCK, toks), jnp.bfloat16),
            pltpu.VMEM((toks, 1), jnp.float32),
        ],
        compiler_params=pltpu.CompilerParams(
            vmem_limit_bytes=48 * MIB, dimension_semantics=("arbitrary",)
        ),
        cost_estimate=pl.CostEstimate(flops=12 * 10**9, bytes_accessed=27 * 10**6, transcendentals=1024),
        name="dispatch",
    )(target, tokens, gain)


def adapter_kernel(aid_ref, *refs):
    xs, refs = refs[:BLOCKS], refs[BLOCKS:]
    downs, refs = refs[: 2 * LINE], refs[2 * LINE :]
    upqs, refs = refs[: 2 * LINE], refs[2 * LINE :]
    upvs, refs = refs[: 2 * LINE], refs[2 * LINE :]
    outs, refs = refs[:BLOCKS], refs[BLOCKS:]
    xbuf, dbuf, qbuf, vbuf, obuf, sem_x, sem_w, sem_o = refs
    rows = BLOCKS * DEVICE_CAP
    qcols, vcols = qbuf.shape[-1], vbuf.shape[-1]

    def x_copy(s, b):
        return pltpu.make_async_copy(
            xs[b].at[pl.ds(pl.multiple_of(s * DEVICE_CAP, DEVICE_CAP), DEVICE_CAP), :],
            xbuf.at[s, pl.ds(b * DEVICE_CAP, DEVICE_CAP), :],
            sem_x.at[s, b],
        )

    def o_copy(s, b):
        return pltpu.make_async_copy(
            obuf.at[s, pl.ds(b * DEVICE_CAP, DEVICE_CAP), :],
            outs[b].at[pl.ds(pl.multiple_of(s * DEVICE_CAP, DEVICE_CAP), DEVICE_CAP), :],
            sem_o.at[s, b],
        )

    def w_copies(s, ref):
        pairs = []
        for h in range(2):
            for i, (src, buf) in enumerate(((downs, dbuf), (upqs, qbuf), (upvs, vbuf))):
                at = src[2 * ref + h]
                at = at.at[pl.ds(2 * h, 2)] if at.shape[0] == 4 else at
                pairs.append(pltpu.make_async_copy(at, buf.at[s, pl.ds(2 * h, 2)], sem_w.at[s, 3 * h + i]))
        return pairs

    for s in range(LINE):
        for b in range(BLOCKS):
            x_copy(s, b).start()
        for copy in w_copies(s, s):
            copy.start()

    def one(s, carry):
        for b in range(BLOCKS):
            x_copy(s, b).wait()
        for copy in w_copies(s, 0):
            copy.wait()
        aid = aid_ref[s]
        x = xbuf[s]
        lane = lax.broadcasted_iota(jnp.int32, (rows, 128), 1)
        low = jnp.zeros((rows, 128), jnp.float32)
        for p in range(2):
            pair = jnp.concatenate([dbuf[s, 2 * p], dbuf[s, 2 * p + 1]], axis=1)
            wide = jnp.dot(x, pair, preferred_element_type=jnp.float32)
            low = jnp.where(aid == 2 * p, wide[:, :128], low)
            low = jnp.where(aid == 2 * p + 1, wide[:, 128:], low)
        turned = pltpu.roll(low, 64, 1)
        low_q = jnp.where(lane < 64, low, turned)
        low_v = jnp.where(lane < 64, turned, low)
        half = jnp.where(lane < 64, 0, 1)

        def spread(values):
            return jnp.concatenate(
                [jnp.where(aid == 2 * p + half, values, 0.0).astype(jnp.bfloat16) for p in range(2)], axis=1
            )

        up_q = qbuf[s].reshape(4 * 64, qcols)
        up_v = vbuf[s].reshape(4 * 64, vcols)
        obuf[s, :, :qcols] = jnp.dot(spread(low_q), up_q, preferred_element_type=jnp.float32).astype(jnp.bfloat16)
        obuf[s, :, qcols:] = jnp.dot(spread(low_v), up_v, preferred_element_type=jnp.float32).astype(jnp.bfloat16)
        for b in range(BLOCKS):
            o_copy(s, b).start()
        return carry

    lax.fori_loop(0, LINE, one, 0)
    for s in range(LINE):
        for b in range(BLOCKS):
            o_copy(s, b).wait()


def adapters(aid, xs, downs, upqs, upvs):
    feats = xs[0].shape[1]
    qcols, vcols = upqs[0].shape[-1], upvs[0].shape[-1]
    rows = BLOCKS * DEVICE_CAP
    anys = pl.BlockSpec(memory_space=pl.ANY)
    return pl.pallas_call(
        adapter_kernel,
        out_shape=(jax.ShapeDtypeStruct((BLOCK, qcols + vcols), jnp.bfloat16),) * BLOCKS,
        in_specs=[pl.BlockSpec(memory_space=pltpu.VMEM)] + [anys] * (BLOCKS + 6 * LINE),
        out_specs=(anys,) * BLOCKS,
        scratch_shapes=[
            pltpu.VMEM((LINE, rows, feats), jnp.bfloat16),
            pltpu.VMEM((LINE, 4, feats, 128), jnp.bfloat16),
            pltpu.VMEM((LINE, 4, 64, qcols), jnp.bfloat16),
            pltpu.VMEM((LINE, 4, 64, vcols), jnp.bfloat16),
            pltpu.VMEM((LINE, rows, qcols + vcols), jnp.bfloat16),
            pltpu.SemaphoreType.DMA((LINE, BLOCKS)),
            pltpu.SemaphoreType.DMA((LINE, 6)),
            pltpu.SemaphoreType.DMA((LINE, BLOCKS)),
        ],
        compiler_params=pltpu.CompilerParams(vmem_limit_bytes=56 * MIB),
        cost_estimate=pl.CostEstimate(flops=8 * 10**9, bytes_accessed=38 * 10**6, transcendentals=0),
        name="adapters",
    )(aid, *xs, *downs, *upqs, *upvs)


def combine_kernel(target_ref, base_ref, *refs):
    deltas, (q_ref, v_ref) = refs[:BLOCKS], refs[BLOCKS:]
    toks = target_ref.shape[0]
    total = None
    for b in range(BLOCKS):
        rows = lax.broadcasted_iota(jnp.int32, (toks, BLOCK), 1) + b * BLOCK
        pick = (rows == target_ref[...]).astype(jnp.float32).astype(jnp.bfloat16)
        part = jnp.dot(pick, deltas[b][...], preferred_element_type=jnp.float32)
        total = part if total is None else total + part
    result = (base_ref[...] + ADAPTER_SCALE * total).astype(jnp.bfloat16)
    qcols = q_ref.shape[1]
    q_ref[...] = result[:, :qcols]
    v_ref[...] = result[:, qcols:]


def combine(target, base, deltas, qcols):
    toks, cols = base.shape
    tile = 128
    return pl.pallas_call(
        combine_kernel,
        grid=(toks // tile,),
        out_shape=(
            jax.ShapeDtypeStruct((toks, qcols), jnp.bfloat16),
            jax.ShapeDtypeStruct((toks, cols - qcols), jnp.bfloat16),
        ),
        in_specs=[
            pl.BlockSpec((tile, 1), lambda i: (i, 0)),
            pl.BlockSpec((tile, cols), lambda i: (i, 0)),
        ]
        + [pl.BlockSpec((BLOCK, cols), lambda i: (0, 0))] * BLOCKS,
        out_specs=(
            pl.BlockSpec((tile, qcols), lambda i: (i, 0)),
            pl.BlockSpec((tile, cols - qcols), lambda i: (i, 0)),
        ),
        compiler_params=pltpu.CompilerParams(
            vmem_limit_bytes=48 * MIB, dimension_semantics=("arbitrary",)
        ),
        cost_estimate=pl.CostEstimate(flops=8 * 10**9, bytes_accessed=21 * 10**6, transcendentals=0),
        name="combine",
    )(target, base, *deltas)


def at(z, y, c):
    return (z % LINE) * 8 + (y % LINE) * 2 + c


def places():
    return [(z, y, c) for z in range(LINE) for y in range(LINE) for c in range(2)]


def row_pairs(cross, d):
    pairs = []
    for z, y, c in places():
        to = c ^ cross
        pairs.append((at(z, y, c), at(z + d, y, to) if to == 0 else at(z, y + d, to)))
    return pairs


def back(pairs):
    return [(j, i) for i, j in pairs]


def line_pairs(s):
    return [(at(z, y + s, c) if c == 0 else at(z + s, y, c), at(z, y, c)) for z, y, c in places()]


def gather_line(shard):
    half = shard.shape[0] // 2
    one = lax.ppermute(shard, "dev", line_pairs(1))
    three = lax.ppermute(shard, "dev", line_pairs(3))
    two_a = lax.ppermute(one[:half], "dev", line_pairs(1))
    two_b = lax.ppermute(three[half:], "dev", line_pairs(3))
    return [shard, shard, one, one, two_a, two_b, three, three]


def body(
    tokens,
    input_norm_gain,
    base_query_value_weight,
    adapter_down_weight,
    adapter_up_query,
    adapter_up_value,
    token_adapter_id,
    adapter_storage_row,
):
    toks = tokens.shape[0]
    pool = adapter_storage_row.shape[0]
    qcols = adapter_up_query.shape[2]
    me = lax.axis_index("dev")
    z, y, c = me // 8, (me // 2) % LINE, me % 2
    weight = lax.all_gather(base_query_value_weight, "grp", axis=0, tiled=True)
    downs = gather_line(adapter_down_weight)
    upqs = gather_line(adapter_up_query)
    upvs = gather_line(adapter_up_value)
    target, counts = plan(
        jnp.stack([z, y, c]).astype(jnp.int32), token_adapter_id.reshape(1, toks), adapter_storage_row.reshape(pool, 1)
    )
    everyone = lax.all_to_all(
        jnp.broadcast_to(counts.reshape(1, pool), (32, pool)), "dev", split_axis=0, concat_axis=0, tiled=True
    )
    normed, *rows = dispatch(target, tokens, input_norm_gain.reshape(1, -1))
    arrived = [
        rows[k * LINE + d] if (k, d) == (0, 0) else lax.ppermute(rows[k * LINE + d], "dev", row_pairs(k, d))
        for k in range(2)
        for d in range(LINE)
    ]
    cross = jnp.arange(BLOCKS) // LINE
    step = jnp.arange(BLOCKS) % LINE
    sender_c = jnp.bitwise_xor(c, cross)
    sender = jnp.where(
        c == 0,
        ((z - step) % LINE) * 8 + y * 2 + sender_c,
        z * 8 + ((y - step) % LINE) * 2 + sender_c,
    )
    sub = jnp.arange(LINE)
    owner = jnp.where(c == 0, z * 8 + ((y + sub) % LINE) * 2, ((z + sub) % LINE) * 8 + y * 2 + 1)
    slot = (owner[:, None] * 4 + jnp.arange(4)[None, :]).reshape(-1)
    pick_sender = (sender[:, None] == jnp.arange(32)[None, :]).astype(jnp.float32)
    pick_slot = (slot[:, None] == jnp.arange(pool)[None, :]).astype(jnp.float32)
    held = jnp.einsum("bd,dp,sp->sb", pick_sender, everyone, pick_slot).reshape(LINE, 4, BLOCKS)
    ends = jnp.stack([held[:, 0], held[:, 0] + held[:, 1], held[:, 0] + held[:, 1] + held[:, 2]], axis=1)
    aid = jnp.sum(
        (ends[..., None] <= jnp.arange(DEVICE_CAP, dtype=jnp.float32)).astype(jnp.int32), axis=1
    ).reshape(LINE, BLOCKS * DEVICE_CAP, 1)
    deltas = adapters(aid, arrived, downs, upqs, upvs)
    returned = [
        deltas[k * LINE + d]
        if (k, d) == (0, 0)
        else lax.ppermute(deltas[k * LINE + d], "dev", back(row_pairs(k, d)))
        for k in range(2)
        for d in range(LINE)
    ]
    base = jnp.dot(normed, weight, preferred_element_type=jnp.float32)
    return combine(target.reshape(toks, 1), base, returned, qcols)


def solution(mesh):
    in_specs = (
        P(("grp", "dev"), None),
        P(),
        P("grp", None),
        P("dev", None, None),
        P("dev", None, None),
        P("dev", None, None),
        P(("grp", "dev"), None),
        P(),
    )
    out_specs = (P(("grp", "dev"), None), P(("grp", "dev"), None))
    return jax.shard_map(body, mesh=mesh, in_specs=in_specs, out_specs=out_specs, check_vma=False)
```

time: 425 us -> 310 us (0.73); the launches traced: 425 us -> 306 us
  waiting for transfers between devices: 297 us -> 141 us
  Pallas kernels: 0 us -> 53.9 us
  starting transfers between devices: 18 us -> 59.7 us
  local copies, waits for them, and re-layouts: 42.5 us -> 11.8 us
  other arithmetic: 17.7 us -> 0.39 us
  matrix products: 35.4 us -> 24.4 us
    all_to_all x3 -> x1, waiting for transfers between devices: 297 us -> 25.5 us  [body(): lax.all_to_all(jnp.broadcast_to(counts.reshape(1, pool), (32, pool)), 'de...]
    ppermute x0 -> x26, waiting for transfers between devices: none -> 115 us  [the longest x3 51.7 us: gather_line(): one = lax.ppermute(shard, 'dev', line_pairs(1))]
    ppermute x0 -> x26, starting transfers between devices: none -> 54.2 us  [the longest x7 28.8 us: body(): lax.ppermute(rows[k * LINE + d], 'dev', row_pairs(k, d))]
    pallas_call x0 -> x4, Pallas kernels: none -> 53.9 us  [the longest x1 21.4 us: dispatch(): pl.pallas_call(dispatch_kernel, grid=(feats // chunk,), out_shape=(jax.Sh...]
    scatter x1 -> x0, local copies, waits for them, and re-layouts: 19.7 us -> none  [body(): jnp.zeros((pool_size * capacity, feature_count), jnp.bfloat16).at[target]]
    gather x2 -> x0, local copies, waits for them, and re-layouts: 17 us -> none  [the longest x1 12 us: body(): delta_q.reshape(pool_size * capacity, query_column_range)[target]]
    all_to_all x3 -> x1, starting transfers between devices: 17.7 us -> 5.47 us  [body(): lax.all_to_all(jnp.broadcast_to(counts.reshape(1, pool), (32, pool)), 'de...]
    convert_element_type x4 -> x0, other arithmetic: 11.1 us -> none  [the longest x1 6.14 us: normalize(): (values * factor * input_norm_gain.astype(jnp.float32)[None, :]).astype(j...]
  transfers between devices with their start and end apart: 4 -> 28, of which waited for: 3 -> 7; matrix products, arithmetic and copies ran while one was open for 8% -> 11% of each run, Pallas kernels for 0% -> 13%
where the time goes in v1:
time: 310 us; the launch traced here: 306 us
  waiting for transfers between devices  141 us (45%)
  starting transfers between devices  59.7 us (19%)
  Pallas kernels  53.9 us (17%)
  matrix products  24.4 us (8%)
  between operations  14.3 us (5%)
  local copies, waits for them, and re-layouts  11.8 us (4%)
    ppermute x3, waiting for transfers between devices, gather_line(): one = lax.ppermute(shard, 'dev', line_pairs(1))  51.7 us
    ppermute x7, waiting for transfers between devices, body(): lax.ppermute(rows[k * LINE + d], 'dev', row_pairs(k, d))  45 us
    ppermute x7, starting transfers between devices, body(): lax.ppermute(rows[k * LINE + d], 'dev', row_pairs(k, d))  28.8 us
    all_to_all x1, waiting for transfers between devices, body(): lax.all_to_all(jnp.broadcast_to(counts.reshape(1, pool), (32, pool)), 'de...  25.5 us
    dot_general x1, matrix products, body(): base = jnp.dot(normed, weight, preferred_element_type=jnp.float32)  24.1 us
    pallas_call x1, Pallas kernels, dispatch(): pl.pallas_call(dispatch_kernel, grid=(feats // chunk,), out_shape=(jax.Sh...  21.4 us
    ppermute x7, waiting for transfers between devices, body(): lax.ppermute(deltas[k * LINE + d], 'dev', back(row_pairs(k, d)))  16.7 us
    pallas_call x1, Pallas kernels, adapters(): pl.pallas_call(adapter_kernel, out_shape=(jax.ShapeDtypeStruct((BLOCK, qc...  16.3 us
  transfers between devices with their start and end apart: 28, of which 7 were waited for; matrix products, arithmetic and copies ran while one was open for 11% of the time, Pallas kernels for 13%

profile of v1, /device:TPU:0, one launch (start us, length us, event | category | flops | bytes accessed | tf_op | source)
XLA Modules:
  0.0 305.7 jit_solution(7879707829232175164)
XLA Ops:
  7.9 1.7 collective-permute-start.9
  11.2 1.9 collective-permute-start.15
  14.8 40.8 %collective-permute-done.15.refs_26_.refs_27_ = bf16[4,64,512]{2,1,0:T(8,128)(2,1)S(1)} collective-permute-done((bf16[4,64,512]{2,1,0:T(8,128)(2,1)S(1)}, bf16[4,64,512]{2,1,0:T(8,128)(2,1)S(1)}, u32[]{:S(2)}, u32[]{:S(2)}) %collective-permute-start.15) | collective-permute-done | bytes 262176 | tf_op jit(solution)/shard_map/ppermute | solution.py:293
  55.6 2.9 collective-permute-start.16
  58.6 21.4 %dispatch.1 = (bf16[1024,3584]{1,0:T(8,128)(2,1)}, bf16[192,3584]{1,0:T(8,128)(2,1)S(1)}, bf16[192,3584]{1,0:T(8,128)(2,1)S(1)}, bf16[192,3584]{1,0:T(8,128)(2,1...) custom-call(s32[1,1024]{1,0:T(1,128)S(1)} %get-tuple-element.21.targ, ...), custom_call_target="tpu_custom_call" | custom-call | flops 12000000000 | bytes 27000000 | tf_op jit(solution)/shard_map/dispatch/pallas_call | solution.py:98
  80.0 2.1 collective-permute-start
  82.1 3.2 %collective-permute-start.11 = (bf16[4,64,1792]{2,1,0:T(8,128)(2,1)S(1)}, bf16[4,64,1792]{2,1,0:T(8,128)(2,1)S(1)}, u32[]{:S(2)}, u32[]{:S(2)}) collective-permute-start(bf16[4,64,1792]{2,1,0:T(8,128)(2,1)S(1)} %copy-done.5), channel_id=1, source_target_pairs={{2,0},{9,1},{4,2},{11,3},{6,4},{13,5},{0,6},{15,7},{10,8},{17,9},{... | collective-permute-start | bytes 2752520 | tf_op jit(solution)/shard_map/ppermute | solution.py:293
  85.3 10.9 %collective-permute-done.11.refs_18_.refs_19_ = bf16[4,64,1792]{2,1,0:T(8,128)(2,1)S(1)} collective-permute-done((bf16[4,64,1792]{2,1,0:T(8,128)(2,1)S(1)}, bf16[4,64,1792]{2,1,0:T(8,128)(2,1)S(1)}, u32[]{:S(2)}, u32[]{:S(2)}) %collective-permute-start.11) | collective-permute-done | bytes 917536 | tf_op jit(solution)/shard_map/ppermute | solution.py:293
  96.2 19.3 %collective-permute-start.1 = (bf16[192,3584]{1,0:T(8,128)(2,1)S(1)}, bf16[192,3584]{1,0:T(8,128)(2,1)S(1)}, u32[]{:S(2)}, u32[]{:S(2)}) collective-permute-start(bf16[192,3584]{1,0:T(8,128)(2,1)S(1)} %get-tuple-element.26), channel_id=1, source_target_pairs={{0,16},{1,5},{2,18},{3,7},{4,20},{5,1},{6,22},{7,3},{8,24},{9,13},... | collective-permute-start | bytes 4128776 | tf_op jit(solution)/shard_map/ppermute | solution.py:327
  117.2 5.8 %collective-permute-start.5 = (bf16[192,3584]{1,0:T(8,128)(2,1)}, bf16[192,3584]{1,0:T(8,128)(2,1)}, u32[]{:S(2)}, u32[]{:S(2)}) collective-permute-start(bf16[192,3584]{1,0:T(8,128)(2,1)} %get-tuple-element.30), channel_id=1, source_target_pairs={{0,5},{1,16},{2,7},{3,18},{4,1},{5,20},{6,3},{7,22},{8,13},{9,24},... | collective-permute-start | bytes 4128776 | tf_op jit(solution)/shard_map/ppermute | solution.py:327
  123.1 2.9 slice.43
  126.0 2.8 slice.42
  128.8 15.5 %collective-permute-done.1.refs_2_ = bf16[192,3584]{1,0:T(8,128)(2,1)S(1)} collective-permute-done((bf16[192,3584]{1,0:T(8,128)(2,1)S(1)}, bf16[192,3584]{1,0:T(8,128)(2,1)S(1)}, u32[]{:S(2)}, u32[]{:S(2)}) %collective-permute-start.1) | collective-permute-done | bytes 1376288 | tf_op jit(solution)/shard_map/ppermute | solution.py:327
  144.3 29.5 %collective-permute-done.2.refs_3_ = bf16[192,3584]{1,0:T(8,128)(2,1)S(1)} collective-permute-done((bf16[192,3584]{1,0:T(8,128)(2,1)S(1)}, bf16[192,3584]{1,0:T(8,128)(2,1)S(1)}, u32[]{:S(2)}, u32[]{:S(2)}) %collective-permute-start.2) | collective-permute-done | bytes 1376288 | tf_op jit(solution)/shard_map/ppermute | solution.py:327
  173.9 3.7 %collective-permute-start.8 = (bf16[2,3584,128]{2,1,0:T(8,128)(2,1)}, bf16[2,3584,128]{2,1,0:T(8,128)(2,1)}, u32[]{:S(2)}, u32[]{:S(2)}) collective-permute-start(bf16[2,3584,128]{2,1,0:T(8,128)(2,1)} %slice.42), channel_id=1, source_target_pairs={{2,0},{9,1},{4,2},{11,3},{6,4},{13,5},{0,6},{15,7},{10,8},{17,9},{... | collective-permute-start | bytes 5505032 | tf_op jit(solution)/shard_map/ppermute | solution.py:295
  179.4 5.5 %all-to-all-start = ((f32[32,1,128]{2,1,0:T(1,128)}), f32[32,1,128]{2,1,0:T(1,128)S(1)}, u32[]{:S(2)}, u32[]{:S(2)}) async-start(f32[32,1,128]{2,1,0:T(1,128)} %broadcast_in_dim.5), calls=%async_computation | async-start | bytes 32768 | tf_op jit(solution)/shard_map/all_to_all | solution.py:322
  186.7 3.0 collective-permute-start.12
  189.7 25.5 %all-to-all-done = f32[32,1,128]{2,1,0:T(1,128)S(1)} async-done(((f32[32,1,128]{2,1,0:T(1,128)}), f32[32,1,128]{2,1,0:T(1,128)S(1)}, u32[]{:S(2)}, u32[]{:S(2)}) %all-to-all-start) | async-done | bytes 16416 | tf_op jit(solution)/shard_map/all_to_all | solution.py:322
  219.4 16.3 %adapters.1 = (bf16[192,2304]{1,0:T(8,128)(2,1)}, bf16[192,2304]{1,0:T(8,128)(2,1)}, bf16[192,2304]{1,0:T(8,128)(2,1)}, bf16[192,2304]{1,0:T(8,128)(2,1)}, bf16[...) custom-call(s32[4,384,1]{2,1,0:T(8,128)} %reshape.142.aid_ref, ...), custom_call_target="tpu_custom_call" | custom-call | flops 8000000000 | bytes 38000000 | tf_op jit(solution)/shard_map/adapters/pallas_call | solution.py:204
  235.7 3.8 %collective-permute-start.19 = (bf16[192,2304]{1,0:T(8,128)(2,1)}, bf16[192,2304]{1,0:T(8,128)(2,1)S(1)}, u32[]{:S(2)}, u32[]{:S(2)}) collective-permute-start(bf16[192,2304]{1,0:T(8,128)(2,1)} %get-tuple-element.33), channel_id=1, source_target_pairs={{8,0},{3,1},{10,2},{5,3},{12,4},{7,5},{14,6},{1,7},{16,8},{11,9},{... | collective-permute-start | bytes 2654216 | tf_op jit(solution)/shard_map/ppermute | solution.py:353
  240.7 2.4 collective-permute-start.23
  243.1 16.7 %collective-permute-done.19.refs_1_ = bf16[192,2304]{1,0:T(8,128)(2,1)S(1)} collective-permute-done((bf16[192,2304]{1,0:T(8,128)(2,1)}, bf16[192,2304]{1,0:T(8,128)(2,1)S(1)}, u32[]{:S(2)}, u32[]{:S(2)}) %collective-permute-start.19) | collective-permute-done | bytes 884768 | tf_op jit(solution)/shard_map/ppermute | solution.py:353
  259.9 24.1 %fusion.23.base_ref = f32[1024,2304]{1,0:T(8,128)} fusion(bf16[1024,3584]{1,0:T(8,128)(2,1)} %get-tuple-element.22, bf16[3584,2304]{1,0:T(8,128)(2,1)} %all-gather.2.cloned.1.call-done), kind=kOutput, calls=%fused_computation.48 | convolution fusion | flops 16911433728 | bytes 33292288 | tf_op jit(solution)/shard_map/dot_general | solution.py:357
  284.0 14.8 %combine.1 = (bf16[1024,1792]{1,0:T(8,128)(2,1)}, bf16[1024,512]{1,0:T(8,128)(2,1)}) custom-call(s32[1024,1]{1,0:T(8,128)S(1)} %copy.19.target_ref, f32[1024,2304]{1,0:T(8,128)} %fusion.23.base_ref, bf16[192,2304]{1,0:T(8,128)(2,1)S(1)} %copy-done.2, bf16[192,2304]{1,0:T(8,128)(2,1)S(1)} %collective-permute-done.19.refs_1_, ...), custom_call_target="tpu_custom_call" | custom-call | flops 8000000000 | bytes 21000000 | tf_op jit(solution)/shard_map/combine/pallas_call | solution.py:243
  (95 shorter events, 14.7 us)
Async XLA Ops:
  7.2 252.7 %all-gather.2.cloned.1.call-start = ((), (), s32[]{:S(2)}) async-start(), calls=%async_computation.1 | async-start | bytes 20643840 | tf_op jit(solution)/shard_map/all_gather | solution.py:315
  7.9 109.2 %collective-permute-start.9 = (bf16[4,3584,128]{2,1,0:T(8,128)(2,1)}, bf16[4,3584,128]{2,1,0:T(8,128)(2,1)}, u32[]{:S(2)}, u32[]{:S(2)}) collective-permute-start(bf16[4,3584,128]{2,1,0:T(8,128)(2,1)} %refs_9_.1), channel_id=1, source_target_pairs={{6,0},{25,1},{0,2},{27,3},{2,4},{29,5},{4,6},{31,7},{14,8},{1,9},{... | collective-permute-start | bytes 11010056 | tf_op jit(solution)/shard_map/ppermute | solution.py:294
  9.7 107.6 %collective-permute-start.7 = (bf16[4,3584,128]{2,1,0:T(8,128)(2,1)}, bf16[4,3584,128]{2,1,0:T(8,128)(2,1)}, u32[]{:S(2)}, u32[]{:S(2)}) collective-permute-start(bf16[4,3584,128]{2,1,0:T(8,128)(2,1)} %refs_9_.1), channel_id=1, source_target_pairs={{2,0},{9,1},{4,2},{11,3},{6,4},{13,5},{0,6},{15,7},{10,8},{17,9},{... | collective-permute-start | bytes 11010056 | tf_op jit(solution)/shard_map/ppermute | solution.py:293
  11.2 44.3 %collective-permute-start.15 = (bf16[4,64,512]{2,1,0:T(8,128)(2,1)S(1)}, bf16[4,64,512]{2,1,0:T(8,128)(2,1)S(1)}, u32[]{:S(2)}, u32[]{:S(2)}) collective-permute-start(bf16[4,64,512]{2,1,0:T(8,128)(2,1)S(1)} %copy-done.12), channel_id=1, source_target_pairs={{2,0},{9,1},{4,2},{11,3},{6,4},{13,5},{0,6},{15,7},{10,8},{17,9},{... | collective-permute-start | bytes 786440 | tf_op jit(solution)/shard_map/ppermute | solution.py:293
  13.1 45.3 %collective-permute-start.17 = (bf16[4,64,512]{2,1,0:T(8,128)(2,1)S(1)}, bf16[4,64,512]{2,1,0:T(8,128)(2,1)S(1)}, u32[]{:S(2)}, u32[]{:S(2)}) collective-permute-start(bf16[4,64,512]{2,1,0:T(8,128)(2,1)S(1)} %copy-done.12), channel_id=1, source_target_pairs={{6,0},{25,1},{0,2},{27,3},{2,4},{29,5},{4,6},{31,7},{14,8},{1,9},{... | collective-permute-start | bytes 786440 | tf_op jit(solution)/shard_map/ppermute | solution.py:294
  55.6 26.5 %collective-permute-start.16 = (bf16[2,64,512]{2,1,0:T(8,128)(2,1)S(1)}, bf16[2,64,512]{2,1,0:T(8,128)(2,1)S(1)}, u32[]{:S(2)}, u32[]{:S(2)}) collective-permute-start(bf16[2,64,512]{2,1,0:T(8,128)(2,1)S(1)} %slice.46), channel_id=1, source_target_pairs={{2,0},{9,1},{4,2},{11,3},{6,4},{13,5},{0,6},{15,7},{10,8},{17,9},{... | collective-permute-start | bytes 393224 | tf_op jit(solution)/shard_map/ppermute | solution.py:295
  58.5 26.9 %collective-permute-start.18 = (bf16[2,64,512]{2,1,0:T(8,128)(2,1)S(1)}, bf16[2,64,512]{2,1,0:T(8,128)(2,1)}, u32[]{:S(2)}, u32[]{:S(2)}) collective-permute-start(bf16[2,64,512]{2,1,0:T(8,128)(2,1)S(1)} %slice.47), channel_id=1, source_target_pairs={{6,0},{25,1},{0,2},{27,3},{2,4},{29,5},{4,6},{31,7},{14,8},{1,9},{... | collective-permute-start | bytes 393224 | tf_op jit(solution)/shard_map/ppermute | solution.py:296
  80.0 37.1 %collective-permute-start = (bf16[192,3584]{1,0:T(8,128)(2,1)S(1)}, bf16[192,3584]{1,0:T(8,128)(2,1)S(1)}, u32[]{:S(2)}, u32[]{:S(2)}) collective-permute-start(bf16[192,3584]{1,0:T(8,128)(2,1)S(1)} %get-tuple-element.25), channel_id=1, source_target_pairs={{0,8},{1,3},{2,10},{3,5},{4,12},{5,7},{6,14},{7,1},{8,16},{9,11},{... | collective-permute-start | bytes 4128776 | tf_op jit(solution)/shard_map/ppermute | solution.py:327
  85.3 30.2 %collective-permute-start.13 = (bf16[4,64,1792]{2,1,0:T(8,128)(2,1)S(1)}, bf16[4,64,1792]{2,1,0:T(8,128)(2,1)S(1)}, u32[]{:S(2)}, u32[]{:S(2)}) collective-permute-start(bf16[4,64,1792]{2,1,0:T(8,128)(2,1)S(1)} %copy-done.5), channel_id=1, source_target_pairs={{6,0},{25,1},{0,2},{27,3},{2,4},{29,5},{4,6},{31,7},{14,8},{1,9},{... | collective-permute-start | bytes 2752520 | tf_op jit(solution)/shard_map/ppermute | solution.py:294
  96.2 48.1 %collective-permute-start.1 = (bf16[192,3584]{1,0:T(8,128)(2,1)S(1)}, bf16[192,3584]{1,0:T(8,128)(2,1)S(1)}, u32[]{:S(2)}, u32[]{:S(2)}) collective-permute-start(bf16[192,3584]{1,0:T(8,128)(2,1)S(1)} %get-tuple-element.26), channel_id=1, source_target_pairs={{0,16},{1,5},{2,18},{3,7},{4,20},{5,1},{6,22},{7,3},{8,24},{9,13},... | collective-permute-start | bytes 4128776 | tf_op jit(solution)/shard_map/ppermute | solution.py:327
  115.6 58.3 %collective-permute-start.2 = (bf16[192,3584]{1,0:T(8,128)(2,1)S(1)}, bf16[192,3584]{1,0:T(8,128)(2,1)S(1)}, u32[]{:S(2)}, u32[]{:S(2)}) collective-permute-start(bf16[192,3584]{1,0:T(8,128)(2,1)S(1)} %get-tuple-element.27), channel_id=1, source_target_pairs={{0,24},{1,7},{2,26},{3,1},{4,28},{5,3},{6,30},{7,5},{8,0},{9,15},{... | collective-permute-start | bytes 4128776 | tf_op jit(solution)/shard_map/ppermute | solution.py:327
  117.1 60.4 %collective-permute-start.3 = (bf16[192,3584]{1,0:T(8,128)(2,1)}, bf16[192,3584]{1,0:T(8,128)(2,1)S(1)}, u32[]{:S(2)}, u32[]{:S(2)}) collective-permute-start(bf16[192,3584]{1,0:T(8,128)(2,1)} %get-tuple-element.28), channel_id=1, source_target_pairs={{0,1},{1,0},{2,3},{3,2},{4,5},{5,4},{6,7},{7,6},{8,9},{9,8},{10,11... | collective-permute-start | bytes 4128776 | tf_op jit(solution)/shard_map/ppermute | solution.py:327
  117.1 69.6 %collective-permute-start.4 = (bf16[192,3584]{1,0:T(8,128)(2,1)}, bf16[192,3584]{1,0:T(8,128)(2,1)}, u32[]{:S(2)}, u32[]{:S(2)}) collective-permute-start(bf16[192,3584]{1,0:T(8,128)(2,1)} %get-tuple-element.29), channel_id=1, source_target_pairs={{0,3},{1,8},{2,5},{3,10},{4,7},{5,12},{6,1},{7,14},{8,11},{9,16},{... | collective-permute-start | bytes 4128776 | tf_op jit(solution)/shard_map/ppermute | solution.py:327
  117.2 72.5 %collective-permute-start.5 = (bf16[192,3584]{1,0:T(8,128)(2,1)}, bf16[192,3584]{1,0:T(8,128)(2,1)}, u32[]{:S(2)}, u32[]{:S(2)}) collective-permute-start(bf16[192,3584]{1,0:T(8,128)(2,1)} %get-tuple-element.30), channel_id=1, source_target_pairs={{0,5},{1,16},{2,7},{3,18},{4,1},{5,20},{6,3},{7,22},{8,13},{9,24},... | collective-permute-start | bytes 4128776 | tf_op jit(solution)/shard_map/ppermute | solution.py:327
  144.3 74.1 %collective-permute-start.10 = (bf16[2,3584,128]{2,1,0:T(8,128)(2,1)}, bf16[2,3584,128]{2,1,0:T(8,128)(2,1)}, u32[]{:S(2)}, u32[]{:S(2)}) collective-permute-start(bf16[2,3584,128]{2,1,0:T(8,128)(2,1)} %slice.43), channel_id=1, source_target_pairs={{6,0},{25,1},{0,2},{27,3},{2,4},{29,5},{4,6},{31,7},{14,8},{1,9},{... | collective-permute-start | bytes 5505032 | tf_op jit(solution)/shard_map/ppermute | solution.py:296
  173.9 44.6 %collective-permute-start.8 = (bf16[2,3584,128]{2,1,0:T(8,128)(2,1)}, bf16[2,3584,128]{2,1,0:T(8,128)(2,1)}, u32[]{:S(2)}, u32[]{:S(2)}) collective-permute-start(bf16[2,3584,128]{2,1,0:T(8,128)(2,1)} %slice.42), channel_id=1, source_target_pairs={{2,0},{9,1},{4,2},{11,3},{6,4},{13,5},{0,6},{15,7},{10,8},{17,9},{... | collective-permute-start | bytes 5505032 | tf_op jit(solution)/shard_map/ppermute | solution.py:295
  178.7 38.3 %collective-permute-start.6 = (bf16[192,3584]{1,0:T(8,128)(2,1)}, bf16[192,3584]{1,0:T(8,128)(2,1)}, u32[]{:S(2)}, u32[]{:S(2)}) collective-permute-start(bf16[192,3584]{1,0:T(8,128)(2,1)} %get-tuple-element.31), channel_id=1, source_target_pairs={{0,7},{1,24},{2,1},{3,26},{4,3},{5,28},{6,5},{7,30},{8,15},{9,0},{... | collective-permute-start | bytes 4128776 | tf_op jit(solution)/shard_map/ppermute | solution.py:327
  179.4 35.9 %all-to-all-start = ((f32[32,1,128]{2,1,0:T(1,128)}), f32[32,1,128]{2,1,0:T(1,128)S(1)}, u32[]{:S(2)}, u32[]{:S(2)}) async-start(f32[32,1,128]{2,1,0:T(1,128)} %broadcast_in_dim.5), calls=%async_computation | async-start | bytes 32768 | tf_op jit(solution)/shard_map/all_to_all | solution.py:322
  186.7 31.7 %collective-permute-start.12 = (bf16[2,64,1792]{2,1,0:T(8,128)(2,1)}, bf16[2,64,1792]{2,1,0:T(8,128)(2,1)S(1)}, u32[]{:S(2)}, u32[]{:S(2)}) collective-permute-start(bf16[2,64,1792]{2,1,0:T(8,128)(2,1)} %slice.44), channel_id=1, source_target_pairs={{2,0},{9,1},{4,2},{11,3},{6,4},{13,5},{0,6},{15,7},{10,8},{17,9},{... | collective-permute-start | bytes 1376264 | tf_op jit(solution)/shard_map/ppermute | solution.py:295
  189.7 28.7 %collective-permute-start.14 = (bf16[2,64,1792]{2,1,0:T(8,128)(2,1)}, bf16[2,64,1792]{2,1,0:T(8,128)(2,1)S(1)}, u32[]{:S(2)}, u32[]{:S(2)}) collective-permute-start(bf16[2,64,1792]{2,1,0:T(8,128)(2,1)} %slice.45), channel_id=1, source_target_pairs={{6,0},{25,1},{0,2},{27,3},{2,4},{29,5},{4,6},{31,7},{14,8},{1,9},{... | collective-permute-start | bytes 1376264 | tf_op jit(solution)/shard_map/ppermute | solution.py:296
  239.7 44.3 %collective-permute-start.21 = (bf16[192,2304]{1,0:T(8,128)(2,1)}, bf16[192,2304]{1,0:T(8,128)(2,1)S(1)}, u32[]{:S(2)}, u32[]{:S(2)}) collective-permute-start(bf16[192,2304]{1,0:T(8,128)(2,1)} %get-tuple-element.35), channel_id=1, source_target_pairs={{24,0},{7,1},{26,2},{1,3},{28,4},{3,5},{30,6},{5,7},{0,8},{15,9},{... | collective-permute-start | bytes 2654216 | tf_op jit(solution)/shard_map/ppermute | solution.py:353
  240.7 43.3 %collective-permute-start.22 = (bf16[192,2304]{1,0:T(8,128)(2,1)}, bf16[192,2304]{1,0:T(8,128)(2,1)}, u32[]{:S(2)}, u32[]{:S(2)}) collective-permute-start(bf16[192,2304]{1,0:T(8,128)(2,1)} %get-tuple-element.36), channel_id=1, source_target_pairs={{1,0},{0,1},{3,2},{2,3},{5,4},{4,5},{7,6},{6,7},{9,8},{8,9},{11,10... | collective-permute-start | bytes 2654216 | tf_op jit(solution)/shard_map/ppermute | solution.py:353
  240.7 43.3 %collective-permute-start.23 = (bf16[192,2304]{1,0:T(8,128)(2,1)}, bf16[192,2304]{1,0:T(8,128)(2,1)}, u32[]{:S(2)}, u32[]{:S(2)}) collective-permute-start(bf16[192,2304]{1,0:T(8,128)(2,1)} %get-tuple-element.37), channel_id=1, source_target_pairs={{3,0},{8,1},{5,2},{10,3},{7,4},{12,5},{1,6},{14,7},{11,8},{16,9},{... | collective-permute-start | bytes 2654216 | tf_op jit(solution)/shard_map/ppermute | solution.py:353
  259.8 24.2 %collective-permute-start.25 = (bf16[192,2304]{1,0:T(8,128)(2,1)}, bf16[192,2304]{1,0:T(8,128)(2,1)}, u32[]{:S(2)}, u32[]{:S(2)}) collective-permute-start(bf16[192,2304]{1,0:T(8,128)(2,1)} %get-tuple-element.39), channel_id=1, source_target_pairs={{7,0},{24,1},{1,2},{26,3},{3,4},{28,5},{5,6},{30,7},{15,8},{0,9},{... | collective-permute-start | bytes 2654216 | tf_op jit(solution)/shard_map/ppermute | solution.py:353
  (22 other events, 585.6 us)
Sparse Core Ops, SparseCore 0:
  9.7 154.3 all-gather.1

commit v2 on v1

v2 whole, which is shorter than its diff:
```python
import functools
import jax
import jax.numpy as jnp
from jax import lax
from jax.experimental import pallas as pl
from jax.experimental.pallas import tpu as pltpu
from jax.sharding import PartitionSpec as P

ADAPTER_SCALE = 0.5
DEVICE_CAP = 48
LINE = 4
BLOCK = LINE * DEVICE_CAP
BLOCKS = 2 * LINE
PIECE = 64 // LINE
TAG = 128
MIB = 1 << 20


def plan_kernel(coord_ref, ids_ref, row_ref, target_ref, local_ref):
    z, y, c = coord_ref[0], coord_ref[1], coord_ref[2]
    pool, toks = row_ref.shape[0], ids_ref.shape[1]
    catalog = lax.broadcasted_iota(jnp.int32, (pool, toks), 0)
    slot = jnp.sum(jnp.where(ids_ref[...] == catalog, row_ref[...], 0), axis=0, keepdims=True)
    chosen = (slot == catalog).astype(jnp.float32)
    chosen16 = chosen.astype(jnp.bfloat16)
    earlier = (
        lax.broadcasted_iota(jnp.int32, (toks, toks), 0) < lax.broadcasted_iota(jnp.int32, (toks, toks), 1)
    ).astype(jnp.float32).astype(jnp.bfloat16)
    before = jnp.dot(chosen16, earlier, preferred_element_type=jnp.float32)
    si = lax.broadcasted_iota(jnp.int32, (pool, pool), 0)
    sj = lax.broadcasted_iota(jnp.int32, (pool, pool), 1)
    lower = jnp.logical_and(lax.shift_right_logical(si, 2) == lax.shift_right_logical(sj, 2), sj < si)
    lower = lower.astype(jnp.float32).astype(jnp.bfloat16)
    offset = jnp.sum(jnp.dot(lower, chosen16, preferred_element_type=jnp.float32), axis=1, keepdims=True)
    rank = jnp.sum(chosen * (before + offset), axis=0, keepdims=True).astype(jnp.int32)
    owner = lax.shift_right_logical(slot, 2)
    owner_z = lax.shift_right_logical(owner, 3)
    owner_y = jnp.bitwise_and(lax.shift_right_logical(owner, 1), 3)
    owner_c = jnp.bitwise_and(owner, 1)
    dz = jnp.bitwise_and(owner_z - z + LINE, 3)
    dy = jnp.bitwise_and(owner_y - y + LINE, 3)
    step = jnp.where(owner_c == 0, dz, dy)
    sub = jnp.where(owner_c == 0, dy, dz)
    cross = jnp.bitwise_xor(owner_c, c)
    target_ref[...] = (cross * LINE + step) * BLOCK + sub * DEVICE_CAP + rank
    local_ref[...] = jnp.bitwise_and(slot, 3).astype(jnp.float32)


def plan(coords, ids, row):
    toks = ids.shape[1]
    return pl.pallas_call(
        plan_kernel,
        out_shape=(
            jax.ShapeDtypeStruct((1, toks), jnp.int32),
            jax.ShapeDtypeStruct((1, toks), jnp.float32),
        ),
        in_specs=[
            pl.BlockSpec(memory_space=pltpu.SMEM),
            pl.BlockSpec(memory_space=pltpu.VMEM),
            pl.BlockSpec(memory_space=pltpu.VMEM),
        ],
        out_specs=(pl.BlockSpec(memory_space=pltpu.VMEM), pl.BlockSpec(memory_space=pltpu.VMEM)),
        compiler_params=pltpu.CompilerParams(vmem_limit_bytes=32 * MIB),
        name="plan",
    )(coords, ids, row)


def dispatch_kernel(target_ref, local_ref, tokens_ref, gain_ref, normed_ref, *rest):
    blocks, (pick, factor, held, sem) = rest[:BLOCKS], rest[BLOCKS:]
    k = pl.program_id(0)
    toks, feats = tokens_ref.shape
    chunk = normed_ref.shape[1]
    last = pl.ds(feats, TAG)

    def copies(cols, step):
        return [
            pltpu.make_async_copy(held.at[pl.ds(b * BLOCK, BLOCK), cols], blocks[b].at[:, cols], sem.at[step, b])
            for b in range(BLOCKS)
        ]

    def columns(step):
        return pl.ds(pl.multiple_of(step * chunk, 128), chunk)

    @pl.when(k == 0)
    def _():
        tags = jnp.broadcast_to(local_ref[...], (TAG, toks)).astype(jnp.bfloat16)
        for b in range(BLOCKS):
            rows = lax.broadcasted_iota(jnp.int32, (BLOCK, toks), 0) + b * BLOCK
            here = (rows == target_ref[...]).astype(jnp.float32).astype(jnp.bfloat16)
            pick[b * BLOCK : (b + 1) * BLOCK, :] = here
            tag = lax.dot_general(here, tags, (((1,), (1,)), ((), ())), preferred_element_type=jnp.float32)
            held[b * BLOCK : (b + 1) * BLOCK, feats:] = tag.astype(jnp.bfloat16)
        for copy in copies(last, feats // chunk):
            copy.start()

        def sums(i, carry):
            part = tokens_ref[pl.ds(pl.multiple_of(i * 128, 128), 128), :].astype(jnp.float32)
            mean = jnp.sum(part * part, axis=1, keepdims=True) / feats
            factor[pl.ds(pl.multiple_of(i * 128, 128), 128), :] = lax.rsqrt(mean + 1e-06)
            return carry

        lax.fori_loop(0, toks // 128, sums, 0)

    cols = columns(k)
    values = tokens_ref[:, cols].astype(jnp.float32)
    gain = gain_ref[:, cols].astype(jnp.float32)
    normed = (values * factor[...] * gain).astype(jnp.bfloat16)
    normed_ref[...] = normed
    held[:, cols] = jnp.dot(pick[...], normed, preferred_element_type=jnp.float32).astype(jnp.bfloat16)
    for copy in copies(cols, k):
        copy.start()

    @pl.when(k == pl.num_programs(0) - 1)
    def _():
        for step in range(feats // chunk):
            for copy in copies(columns(step), step):
                copy.wait()
        for copy in copies(last, feats // chunk):
            copy.wait()


def dispatch(target, local, tokens, gain):
    toks, feats = tokens.shape
    chunk = 512
    return pl.pallas_call(
        dispatch_kernel,
        grid=(feats // chunk,),
        out_shape=(jax.ShapeDtypeStruct((toks, feats), jnp.bfloat16),)
        + (jax.ShapeDtypeStruct((BLOCK, feats + TAG), jnp.bfloat16),) * BLOCKS,
        in_specs=[
            pl.BlockSpec((1, toks), lambda k: (0, 0)),
            pl.BlockSpec((1, toks), lambda k: (0, 0)),
            pl.BlockSpec((toks, feats), lambda k: (0, 0)),
            pl.BlockSpec((1, feats), lambda k: (0, 0)),
        ],
        out_specs=(pl.BlockSpec((toks, chunk), lambda k: (0, k)),) + (pl.BlockSpec(memory_space=pl.ANY),) * BLOCKS,
        scratch_shapes=[
            pltpu.VMEM((BLOCKS * BLOCK, toks), jnp.bfloat16),
            pltpu.VMEM((toks, 1), jnp.float32),
            pltpu.VMEM((BLOCKS * BLOCK, feats + TAG), jnp.bfloat16),
            pltpu.SemaphoreType.DMA((feats // chunk + 1, BLOCKS)),
        ],
        compiler_params=pltpu.CompilerParams(
            vmem_limit_bytes=56 * MIB, dimension_semantics=("arbitrary",)
        ),
        cost_estimate=pl.CostEstimate(flops=12 * 10**9, bytes_accessed=27 * 10**6, transcendentals=1024),
        name="dispatch",
    )(target, local, tokens, gain)


def adapter_kernel(qcols, count, *refs):
    xs, refs = refs[:count], refs[count:]
    downs, refs = refs[: 2 * LINE], refs[2 * LINE :]
    up_own, up_far, refs = refs[0], refs[1], refs[2:]
    outs, refs = refs[:count], refs[count:]
    xbuf, dbuf, ubuf, obuf, sem_x, sem_w, sem_o = refs
    rows = count * DEVICE_CAP

    def x_copy(s, b):
        return pltpu.make_async_copy(
            xs[b].at[pl.ds(pl.multiple_of(s * DEVICE_CAP, DEVICE_CAP), DEVICE_CAP), :],
            xbuf.at[s, pl.ds(b * DEVICE_CAP, DEVICE_CAP), :],
            sem_x.at[s, b],
        )

    def o_copy(s, b):
        return pltpu.make_async_copy(
            obuf.at[s, pl.ds(b * DEVICE_CAP, DEVICE_CAP), :],
            outs[b].at[pl.ds(pl.multiple_of(s * DEVICE_CAP, DEVICE_CAP), DEVICE_CAP), :],
            sem_o.at[s, b],
        )

    def w_copies(s, ref):
        pairs = []
        for p in range(LINE):
            part = pl.ds(p * PIECE, PIECE)
            src = up_own.at[:, part, :] if ref == 0 else up_far.at[p, ref - 1]
            pairs.append(pltpu.make_async_copy(src, ubuf.at[s, :, part, :], sem_w.at[s, 2 + p]))
        for h in range(2):
            src = downs[2 * ref + h]
            src = src.at[pl.ds(2 * h, 2)] if src.shape[0] == 4 else src
            pairs.append(pltpu.make_async_copy(src, dbuf.at[s, pl.ds(2 * h, 2)], sem_w.at[s, h]))
        return pairs

    for s in range(LINE):
        for b in range(count):
            x_copy(s, b).start()
        for copy in w_copies(s, s):
            copy.start()

    def one(s, carry):
        for b in range(count):
            x_copy(s, b).wait()
        for copy in w_copies(s, 0):
            copy.wait()
        x = xbuf[s, :, : dbuf.shape[2]]
        aid = xbuf[s, :, dbuf.shape[2] :].astype(jnp.float32)
        lane = lax.broadcasted_iota(jnp.int32, (rows, 128), 1)
        low = jnp.zeros((rows, 128), jnp.float32)
        for p in range(2):
            pair = jnp.concatenate([dbuf[s, 2 * p], dbuf[s, 2 * p + 1]], axis=1)
            wide = jnp.dot(x, pair, preferred_element_type=jnp.float32)
            low = jnp.where(aid == 2 * p, wide[:, :128], low)
            low = jnp.where(aid == 2 * p + 1, wide[:, 128:], low)
        turned = pltpu.roll(low, 64, 1)
        low_q = jnp.where(lane < 64, low, turned)
        low_v = jnp.where(lane < 64, turned, low)
        half = jnp.where(lane < 64, 0.0, 1.0)

        def spread(values):
            return jnp.concatenate(
                [jnp.where(aid == 2 * p + half, values, 0.0).astype(jnp.bfloat16) for p in range(2)], axis=1
            )

        up = ubuf[s].reshape(4 * 64, ubuf.shape[-1])
        up_q, up_v = up[:, :qcols], up[:, qcols:]
        obuf[s, :, :qcols] = jnp.dot(spread(low_q), up_q, preferred_element_type=jnp.float32).astype(jnp.bfloat16)
        obuf[s, :, qcols:] = jnp.dot(spread(low_v), up_v, preferred_element_type=jnp.float32).astype(jnp.bfloat16)
        for b in range(count):
            o_copy(s, b).start()
        return carry

    lax.fori_loop(0, LINE, one, 0)
    for s in range(LINE):
        for b in range(count):
            o_copy(s, b).wait()


def adapters(xs, downs, up_own, up_far, qcols):
    feats = downs[0].shape[1]
    cols = up_own.shape[-1]
    count = len(xs)
    rows = count * DEVICE_CAP
    anys = pl.BlockSpec(memory_space=pl.ANY)
    return pl.pallas_call(
        functools.partial(adapter_kernel, qcols, count),
        out_shape=(jax.ShapeDtypeStruct((BLOCK, cols), jnp.bfloat16),) * count,
        in_specs=[anys] * (count + 2 * LINE + 2),
        out_specs=(anys,) * count,
        scratch_shapes=[
            pltpu.VMEM((LINE, rows, feats + TAG), jnp.bfloat16),
            pltpu.VMEM((LINE, 4, feats, 128), jnp.bfloat16),
            pltpu.VMEM((LINE, 4, 64, cols), jnp.bfloat16),
            pltpu.VMEM((LINE, rows, cols), jnp.bfloat16),
            pltpu.SemaphoreType.DMA((LINE, count)),
            pltpu.SemaphoreType.DMA((LINE, 6)),
            pltpu.SemaphoreType.DMA((LINE, count)),
        ],
        compiler_params=pltpu.CompilerParams(vmem_limit_bytes=56 * MIB),
        cost_estimate=pl.CostEstimate(flops=4 * 10**9, bytes_accessed=29 * 10**6, transcendentals=0),
        name="adapters",
    )(*xs, *downs, up_own, up_far)


def combine_kernel(coord_ref, target_ref, mine_ref, theirs_ref, *refs):
    deltas, (q_ref, v_ref, held, sem) = refs[:BLOCKS], refs[BLOCKS:]
    toks, rows = target_ref.shape[0], BLOCKS * BLOCK

    @pl.when(pl.program_id(0) == 0)
    def _():
        copies = [
            pltpu.make_async_copy(deltas[b], held.at[pl.ds(b * BLOCK, BLOCK), :], sem.at[b]) for b in range(BLOCKS)
        ]
        for copy in copies:
            copy.start()
        for copy in copies:
            copy.wait()

    row = lax.broadcasted_iota(jnp.int32, (toks, rows), 1)
    pick = (row == target_ref[...]).astype(jnp.float32).astype(jnp.bfloat16)
    total = jnp.dot(pick, held[...], preferred_element_type=jnp.float32)
    first = coord_ref[2] == 0
    low = jnp.where(first, mine_ref[...], theirs_ref[...])
    high = jnp.where(first, theirs_ref[...], mine_ref[...])
    half, qcols = low.shape[1], q_ref.shape[1]
    low = (low + ADAPTER_SCALE * total[:, :half]).astype(jnp.bfloat16)
    high = (high + ADAPTER_SCALE * total[:, half:]).astype(jnp.bfloat16)
    q_ref[:, :half] = low
    q_ref[:, half:] = high[:, : qcols - half]
    v_ref[...] = high[:, qcols - half :]


def combine(coords, target, mine, theirs, deltas, qcols):
    toks, half = mine.shape
    cols = 2 * half
    tile = 512
    return pl.pallas_call(
        combine_kernel,
        grid=(toks // tile,),
        out_shape=(
            jax.ShapeDtypeStruct((toks, qcols), jnp.bfloat16),
            jax.ShapeDtypeStruct((toks, cols - qcols), jnp.bfloat16),
        ),
        in_specs=[
            pl.BlockSpec(memory_space=pltpu.SMEM),
            pl.BlockSpec((tile, 1), lambda i: (i, 0)),
            pl.BlockSpec((tile, half), lambda i: (i, 0)),
            pl.BlockSpec((tile, half), lambda i: (i, 0)),
        ]
        + [pl.BlockSpec(memory_space=pl.ANY)] * BLOCKS,
        out_specs=(
            pl.BlockSpec((tile, qcols), lambda i: (i, 0)),
            pl.BlockSpec((tile, cols - qcols), lambda i: (i, 0)),
        ),
        scratch_shapes=[
            pltpu.VMEM((BLOCKS * BLOCK, cols), jnp.bfloat16),
            pltpu.SemaphoreType.DMA((BLOCKS,)),
        ],
        compiler_params=pltpu.CompilerParams(
            vmem_limit_bytes=48 * MIB, dimension_semantics=("arbitrary",)
        ),
        cost_estimate=pl.CostEstimate(flops=8 * 10**9, bytes_accessed=21 * 10**6, transcendentals=0),
        name="combine",
    )(coords, target, mine, theirs, *deltas)


def at(z, y, c):
    return (z % LINE) * 8 + (y % LINE) * 2 + c


def places():
    return [(z, y, c) for z in range(LINE) for y in range(LINE) for c in range(2)]


def row_pairs(cross, d):
    pairs = []
    for z, y, c in places():
        to = c ^ cross
        pairs.append((at(z, y, c), at(z + d, y, to) if to == 0 else at(z, y + d, to)))
    return pairs


def back(pairs):
    return [(j, i) for i, j in pairs]


def line_pairs(s):
    return [(at(z, y + s, c) if c == 0 else at(z + s, y, c), at(z, y, c)) for z, y, c in places()]


def line(shard, s):
    return lax.ppermute(shard, "dev", line_pairs(s))


def body(
    tokens,
    input_norm_gain,
    base_query_value_weight,
    adapter_down_weight,
    adapter_up_query,
    adapter_up_value,
    token_adapter_id,
    adapter_storage_row,
):
    toks = tokens.shape[0]
    pool = adapter_storage_row.shape[0]
    qcols = adapter_up_query.shape[2]
    me = lax.axis_index("dev")
    z, y, c = me // 8, (me // 2) % LINE, me % 2
    coords = jnp.stack([z, y, c]).astype(jnp.int32)
    half = adapter_down_weight.shape[0] // 2
    one, three = line(adapter_down_weight, 1), line(adapter_down_weight, 3)
    up = jnp.concatenate([adapter_up_query, adapter_up_value], axis=2)
    piece = lax.dynamic_slice_in_dim(up, lax.axis_index("grp") * PIECE, PIECE, axis=1)
    pieces = jnp.stack([line(piece, s) for s in range(1, LINE)])
    up_far = lax.all_gather(pieces, "grp", axis=0)
    target, local = plan(coords, token_adapter_id.reshape(1, toks), adapter_storage_row.reshape(pool, 1))
    normed, *rows = dispatch(target, local, tokens, input_norm_gain.reshape(1, -1))
    own, other = rows[:LINE], rows[LINE:]
    other[0] = lax.ppermute(other[0], "dev", row_pairs(1, 0))
    own = [own[0]] + [lax.ppermute(own[d], "dev", row_pairs(0, d)) for d in range(1, LINE)]
    one, three, other[0] = lax.optimization_barrier((one, three, other[0]))
    two_a, two_b = line(one[:half], 1), line(three[half:], 3)
    width = base_query_value_weight.shape[1] // 2
    weight = lax.dynamic_slice_in_dim(base_query_value_weight, c * width, width, axis=1)
    other, own[1], weight, up_far = lax.optimization_barrier((other, own[1], weight, up_far))
    mine = lax.all_gather(weight, "grp", axis=0, tiled=True)
    other = [other[0]] + [lax.ppermute(other[d], "dev", row_pairs(1, d)) for d in range(1, LINE)]
    downs = [adapter_down_weight, adapter_down_weight, one, one, two_a, two_b, three, three]
    own = adapters(own, downs, up, up_far, qcols)
    other, _ = lax.optimization_barrier((other, own))
    own = [own[0]] + [lax.ppermute(own[d], "dev", back(row_pairs(0, d))) for d in range(1, LINE)]
    other = adapters(other, downs, up, up_far, qcols)
    other, own[1], own[3], mine = lax.optimization_barrier((list(other), own[1], own[3], mine))
    other = [lax.ppermute(other[d], "dev", back(row_pairs(1, d))) for d in range(LINE)]
    theirs = lax.ppermute(mine, "dev", [(i, i ^ 1) for i in range(32)])
    mine = jnp.dot(normed, mine, preferred_element_type=jnp.float32)
    theirs = jnp.dot(normed, theirs, preferred_element_type=jnp.float32)
    return combine(coords, target.reshape(toks, 1), mine, theirs, own + other, qcols)


def solution(mesh):
    in_specs = (
        P(("grp", "dev"), None),
        P(),
        P("grp", None),
        P("dev", None, None),
        P("dev", None, None),
        P("dev", None, None),
        P(("grp", "dev"), None),
        P(),
    )
    out_specs = (P(("grp", "dev"), None), P(("grp", "dev"), None))
    return jax.shard_map(body, mesh=mesh, in_specs=in_specs, out_specs=out_specs, check_vma=False)
```

time: 310 us -> 249 us (0.80); the launches traced: 306 us -> 248 us
  waiting for transfers between devices: 141 us -> 92.8 us
  starting transfers between devices: 59.7 us -> 32.1 us
  Pallas kernels: 53.9 us -> 61.9 us
  matrix products: 24.4 us -> 31.4 us
    all_to_all x1 -> x0, waiting for transfers between devices: 25.5 us -> none  [body(): lax.all_to_all(jnp.broadcast_to(counts.reshape(1, pool), (32, pool)), 'de...]
    ppermute x26 -> x22, waiting for transfers between devices: 115 us -> 92.7 us  [the longest x3 52.2 us: body(): lax.ppermute(own[d], 'dev', row_pairs(0, d))]
    ppermute x26 -> x22, starting transfers between devices: 54.2 us -> 32 us  [the longest x7 9.72 us: line(): return lax.ppermute(shard, 'dev', line_pairs(s))]
    dot_general x2, matrix products: 24.4 us -> 31.4 us  [the longest x1 15.7 us: body(): mine = jnp.dot(normed, mine, preferred_element_type=jnp.float32)]
    pallas_call x1 -> x2, Pallas kernels: 16.3 us -> 23.3 us  [adapters(): pl.pallas_call(functools.partial(adapter_kernel, qcols, count), out_shape...]
    all_to_all x1 -> x0, starting transfers between devices: 5.47 us -> none  [body(): lax.all_to_all(jnp.broadcast_to(counts.reshape(1, pool), (32, pool)), 'de...]
    slice x6 -> x2, local copies, waits for them, and re-layouts: 7.45 us -> 3.24 us  [body(): two_a, two_b = (line(one[:half], 1), line(three[half:], 3))]
    unnamed x36 -> x39, local copies, waits for them, and re-layouts: 2.06 us -> 6.21 us
  transfers between devices with their start and end apart: 28 -> 24, of which waited for: 7 -> 9; matrix products, arithmetic and copies ran while one was open for 11% -> 16% of each run, Pallas kernels for 13% -> 19%
where the time goes in v2:
time: 249 us; the launch traced here: 248 us
  waiting for transfers between devices  92.8 us (37%)
  Pallas kernels  61.9 us (25%)
  starting transfers between devices  32.1 us (13%)
  matrix products  31.4 us (13%)
  local copies, waits for them, and re-layouts  14.5 us (6%)
  between operations  14.3 us (6%)
    ppermute x3, waiting for transfers between devices, body(): lax.ppermute(own[d], 'dev', row_pairs(0, d))  52.2 us
    ppermute x7, waiting for transfers between devices, line(): return lax.ppermute(shard, 'dev', line_pairs(s))  32 us
    pallas_call x1, Pallas kernels, dispatch(): pl.pallas_call(dispatch_kernel, grid=(feats // chunk,), out_shape=(jax.Sh...  23.6 us
    pallas_call x2, Pallas kernels, adapters(): pl.pallas_call(functools.partial(adapter_kernel, qcols, count), out_shape...  23.3 us
    dot_general x1, matrix products, body(): mine = jnp.dot(normed, mine, preferred_element_type=jnp.float32)  15.7 us
    dot_general x1, matrix products, body(): theirs = jnp.dot(normed, theirs, preferred_element_type=jnp.float32)  15.6 us
    pallas_call x1, Pallas kernels, combine(): pl.pallas_call(combine_kernel, grid=(toks // tile,), out_shape=(jax.Shape...  13.7 us
    ppermute x7, starting transfers between devices, line(): return lax.ppermute(shard, 'dev', line_pairs(s))  9.72 us
  transfers between devices with their start and end apart: 24, of which 9 were waited for; matrix products, arithmetic and copies ran while one was open for 16% of the time, Pallas kernels for 19%

profile of v2, /device:TPU:0, one launch (start us, length us, event | category | flops | bytes accessed | tf_op | source)
XLA Modules:
  0.0 248.0 jit_solution(6006418942739681173)
XLA Ops:
  9.5 3.2 %collective-permute-start.4 = (bf16[4,16,2304]{2,1,0:T(8,128)(2,1)S(1)}, bf16[4,16,2304]{2,1,0:T(8,128)(2,1)S(1)}, u32[]{:S(2)}, u32[]{:S(2)}) collective-permute-start(bf16[4,16,2304]{2,1,0:T(8,128)(2,1)S(1)} %constant_dynamic-slice_fusion), channel_id=1, source_target_pairs={{2,0},{9,1},{4,2},{11,3},{6,4},{13,5},{0,6},{15,7},{10,8},{17,9},{... | collective-permute-start | bytes 884744 | tf_op jit(solution)/shard_map/ppermute | solution.py:342
  14.3 5.8 %collective-permute-done.4 = bf16[4,16,2304]{2,1,0:T(8,128)(2,1)S(1)} collective-permute-done((bf16[4,16,2304]{2,1,0:T(8,128)(2,1)S(1)}, bf16[4,16,2304]{2,1,0:T(8,128)(2,1)S(1)}, u32[]{:S(2)}, u32[]{:S(2)}) %collective-permute-start.4) | collective-permute-done | bytes 294944 | tf_op jit(solution)/shard_map/ppermute | solution.py:342
  21.0 3.1 %collective-permute-done.6 = bf16[4,16,2304]{2,1,0:T(8,128)(2,1)S(1)} collective-permute-done((bf16[4,16,2304]{2,1,0:T(8,128)(2,1)S(1)}, bf16[4,16,2304]{2,1,0:T(8,128)(2,1)S(1)}, u32[]{:S(2)}, u32[]{:S(2)}) %collective-permute-start.6) | collective-permute-done | bytes 294944 | tf_op jit(solution)/shard_map/ppermute | solution.py:342
  30.5 23.6 %dispatch.1 = (bf16[1024,3584]{1,0:T(8,128)(2,1)}, bf16[192,3712]{1,0:T(8,128)(2,1)}, bf16[192,3712]{1,0:T(8,128)(2,1)}, bf16[192,3712]{1,0:T(8,128)(2,1)}, bf16...) custom-call(s32[1,1024]{1,0:T(1,128)} %copy-done, ...), custom_call_target="tpu_custom_call" | custom-call | flops 12000000000 | bytes 27000000 | tf_op jit(solution)/shard_map/dispatch/pallas_call | solution.py:125
  54.2 2.0 collective-permute-start.3
  56.3 3.1 %constant_dynamic-slice_fusion.1 = bf16[896,1152]{1,0:T(8,128)(2,1)} fusion(bf16[896,2304]{1,0:T(8,128)(2,1)} %param.10, s32[]{:T(128)S(6)} %select_n.28), kind=kLoop, calls=%fused_computation.5 | loop fusion | bytes 4128772 | tf_op jit(solution)/shard_map/dynamic_slice | solution.py:375
  59.4 9.1 %collective-permute-done.refs_6_.refs_7_ = bf16[4,3584,128]{2,1,0:T(8,128)(2,1)} collective-permute-done((bf16[4,3584,128]{2,1,0:T(8,128)(2,1)}, bf16[4,3584,128]{2,1,0:T(8,128)(2,1)}, u32[]{:S(2)}, u32[]{:S(2)}) %collective-permute-start) | collective-permute-done | bytes 3670048 | tf_op jit(solution)/shard_map/ppermute | solution.py:342
  68.4 13.1 %collective-permute-done.1.refs_10_.refs_11_ = bf16[4,3584,128]{2,1,0:T(8,128)(2,1)} collective-permute-done((bf16[4,3584,128]{2,1,0:T(8,128)(2,1)}, bf16[4,3584,128]{2,1,0:T(8,128)(2,1)}, u32[]{:S(2)}, u32[]{:S(2)}) %collective-permute-start.1) | collective-permute-done | bytes 3670048 | tf_op jit(solution)/shard_map/ppermute | solution.py:342
  81.6 2.3 collective-permute-done.3.refs_1_
  86.6 1.6 slice.6
  88.2 2.8 %collective-permute-start.12 = (bf16[2,3584,128]{2,1,0:T(8,128)(2,1)S(1)}, bf16[2,3584,128]{2,1,0:T(8,128)(2,1)S(1)}, u32[]{:S(2)}, u32[]{:S(2)}) collective-permute-start(bf16[2,3584,128]{2,1,0:T(8,128)(2,1)S(1)} %slice.6), channel_id=1, source_target_pairs={{2,0},{9,1},{4,2},{11,3},{6,4},{13,5},{0,6},{15,7},{10,8},{17,9},{... | collective-permute-start | bytes 5505032 | tf_op jit(solution)/shard_map/ppermute | solution.py:342
  91.0 1.6 slice.7
  94.0 17.8 %collective-permute-done.10.refs_2_ = bf16[192,3712]{1,0:T(8,128)(2,1)S(1)} collective-permute-done((bf16[192,3712]{1,0:T(8,128)(2,1)}, bf16[192,3712]{1,0:T(8,128)(2,1)S(1)}, u32[]{:S(2)}, u32[]{:S(2)}) %collective-permute-start.10) | collective-permute-done | bytes 1425440 | tf_op jit(solution)/shard_map/ppermute | solution.py:371
  113.0 32.1 %collective-permute-done.11.refs_3_ = bf16[192,3712]{1,0:T(8,128)(2,1)S(1)} collective-permute-done((bf16[192,3712]{1,0:T(8,128)(2,1)}, bf16[192,3712]{1,0:T(8,128)(2,1)S(1)}, u32[]{:S(2)}, u32[]{:S(2)}) %collective-permute-start.11) | collective-permute-done | bytes 1425440 | tf_op jit(solution)/shard_map/ppermute | solution.py:371
  147.4 11.6 %adapters.2 = (bf16[192,2304]{1,0:T(8,128)(2,1)}, bf16[192,2304]{1,0:T(8,128)(2,1)}, bf16[192,2304]{1,0:T(8,128)(2,1)}, bf16[192,2304]{1,0:T(8,128)(2,1)}) custom-call(bf16[192,3712]{1,0:T(8,128)(2,1)} %get-tuple-element.55.refs_0_, bf16[192,3712]{1,0:T(8,128)(2,1)} %copy-done.9, bf16[192,3712]{1,0:T(8,128)(2,1)} %copy-done.11, ...), custom_call_target="tpu_custom_call" | custom-call | flops 4000000000 | bytes 29000000 | tf_op jit(solution)/shard_map/adapters/pallas_call | solution.py:235
  159.0 5.9 %collective-permute-start.14 = (bf16[192,2304]{1,0:T(8,128)(2,1)}, bf16[192,2304]{1,0:T(8,128)(2,1)S(1)}, u32[]{:S(2)}, u32[]{:S(2)}) collective-permute-start(bf16[192,2304]{1,0:T(8,128)(2,1)} %get-tuple-element.63), channel_id=1, source_target_pairs={{8,0},{3,1},{10,2},{5,3},{12,4},{7,5},{14,6},{1,7},{16,8},{11,9},{... | collective-permute-start | bytes 2654216 | tf_op jit(solution)/shard_map/ppermute | solution.py:382
  165.0 8.5 %collective-permute-done.9.refs_3_ = bf16[192,3712]{1,0:T(8,128)(2,1)} collective-permute-done((bf16[192,3712]{1,0:T(8,128)(2,1)}, bf16[192,3712]{1,0:T(8,128)(2,1)}, u32[]{:S(2)}, u32[]{:S(2)}) %collective-permute-start.9) | collective-permute-done | bytes 1425440 | tf_op jit(solution)/shard_map/ppermute | solution.py:378
  173.5 11.7 %adapters.3 = (bf16[192,2304]{1,0:T(8,128)(2,1)}, bf16[192,2304]{1,0:T(8,128)(2,1)}, bf16[192,2304]{1,0:T(8,128)(2,1)}, bf16[192,2304]{1,0:T(8,128)(2,1)}) custom-call(bf16[192,3712]{1,0:T(8,128)(2,1)} %copy-done.8, bf16[192,3712]{1,0:T(8,128)(2,1)} %copy-done.10, bf16[192,3712]{1,0:T(8,128)(2,1)} %collective-permute-done.8.refs_2_, ...), custom_call_target="tpu_custom_call" | custom-call | flops 4000000000 | bytes 29000000 | tf_op jit(solution)/shard_map/adapters/pallas_call | solution.py:235
  186.0 3.5 %collective-permute-start.17 = (bf16[192,2304]{1,0:T(8,128)(2,1)S(1)}, bf16[192,2304]{1,0:T(8,128)(2,1)S(1)}, u32[]{:S(2)}, u32[]{:S(2)}) collective-permute-start(bf16[192,2304]{1,0:T(8,128)(2,1)S(1)} %copy-done.15), channel_id=1, source_target_pairs={{16,0},{5,1},{18,2},{7,3},{20,4},{1,5},{22,6},{3,7},{24,8},{13,9},... | collective-permute-start | bytes 2654216 | tf_op jit(solution)/shard_map/ppermute | solution.py:382
  190.3 1.7 collective-permute-start.19
  192.0 1.8 collective-permute-start.20
  193.8 15.7 %fusion.mine_ref = f32[1024,1152]{1,0:T(8,128)} fusion(bf16[1024,3584]{1,0:T(8,128)(2,1)} %get-tuple-element.44, bf16[3584,1152]{1,0:T(8,128)(2,1)} %all-gather.4.cloned.1.call-done), kind=kOutput, calls=%fused_computation.6 | convolution fusion | flops 8455716864 | bytes 20316160 | tf_op jit(solution)/shard_map/dot_general | solution.py:387
  209.9 15.6 %fusion.1.theirs_ref = f32[1024,1152]{1,0:T(8,128)} fusion(bf16[1024,3584]{1,0:T(8,128)(2,1)} %get-tuple-element.44, bf16[3584,1152]{1,0:T(8,128)(2,1)} %collective-permute-done.16), kind=kOutput, calls=%fused_computation.7 | convolution fusion | flops 8455716864 | bytes 20316160 | tf_op jit(solution)/shard_map/dot_general | solution.py:388
  227.4 13.7 %combine.1 = (bf16[1024,1792]{1,0:T(8,128)(2,1)}, bf16[1024,512]{1,0:T(8,128)(2,1)}) custom-call(s32[3]{0:T(128)S(1)} %pad_add_fusion.coord_ref, s32[1024,1]{1,0:T(8,128)S(1)} %copy.14.target_ref, f32[1024,1152]{1,0:T(8,128)} %fusion.mine_ref, f32[1024,1152]{1,0:T(8,128)} %fusion.1.theirs_ref, bf16[192,2304]{1,0:T(8,128)(2,1)S(1)} %copy-done.3, ...), custom_call_target="tpu_custom_call" | custom-call | flops 8000000000 | bytes 21000000 | tf_op jit(solution)/shard_map/combine/pallas_call | solution.py:287
  (82 shorter events, 22.7 us)
Async XLA Ops:
  7.2 76.7 %all-gather.6.cloned.1.call-start = ((), (), s32[]{:S(2)}) async-start(), calls=%async_computation.1 | async-start | bytes 4423680 | tf_op jit(solution)/shard_map/all_gather | solution.py:366
  9.5 10.6 %collective-permute-start.4 = (bf16[4,16,2304]{2,1,0:T(8,128)(2,1)S(1)}, bf16[4,16,2304]{2,1,0:T(8,128)(2,1)S(1)}, u32[]{:S(2)}, u32[]{:S(2)}) collective-permute-start(bf16[4,16,2304]{2,1,0:T(8,128)(2,1)S(1)} %constant_dynamic-slice_fusion), channel_id=1, source_target_pairs={{2,0},{9,1},{4,2},{11,3},{6,4},{13,5},{0,6},{15,7},{10,8},{17,9},{... | collective-permute-start | bytes 884744 | tf_op jit(solution)/shard_map/ppermute | solution.py:342
  12.7 8.3 %collective-permute-start.5 = (bf16[4,16,2304]{2,1,0:T(8,128)(2,1)S(1)}, bf16[4,16,2304]{2,1,0:T(8,128)(2,1)S(1)}, u32[]{:S(2)}, u32[]{:S(2)}) collective-permute-start(bf16[4,16,2304]{2,1,0:T(8,128)(2,1)S(1)} %constant_dynamic-slice_fusion), channel_id=1, source_target_pairs={{4,0},{17,1},{6,2},{19,3},{0,4},{21,5},{2,6},{23,7},{12,8},{25,9},... | collective-permute-start | bytes 884744 | tf_op jit(solution)/shard_map/ppermute | solution.py:342
  13.3 10.8 %collective-permute-start.6 = (bf16[4,16,2304]{2,1,0:T(8,128)(2,1)S(1)}, bf16[4,16,2304]{2,1,0:T(8,128)(2,1)S(1)}, u32[]{:S(2)}, u32[]{:S(2)}) collective-permute-start(bf16[4,16,2304]{2,1,0:T(8,128)(2,1)S(1)} %constant_dynamic-slice_fusion), channel_id=1, source_target_pairs={{6,0},{25,1},{0,2},{27,3},{2,4},{29,5},{4,6},{31,7},{14,8},{1,9},{... | collective-permute-start | bytes 884744 | tf_op jit(solution)/shard_map/ppermute | solution.py:342
  25.1 160.1 %all-gather.4.cloned.1.call-start = ((), (), s32[]{:S(2)}) async-start(), calls=%async_computation | async-start | bytes 10321920 | tf_op jit(solution)/shard_map/all_gather | solution.py:377
  25.2 43.3 %collective-permute-start = (bf16[4,3584,128]{2,1,0:T(8,128)(2,1)}, bf16[4,3584,128]{2,1,0:T(8,128)(2,1)}, u32[]{:S(2)}, u32[]{:S(2)}) collective-permute-start(bf16[4,3584,128]{2,1,0:T(8,128)(2,1)} %refs_5_.3), channel_id=1, source_target_pairs={{2,0},{9,1},{4,2},{11,3},{6,4},{13,5},{0,6},{15,7},{10,8},{17,9},{... | collective-permute-start | bytes 11010056 | tf_op jit(solution)/shard_map/ppermute | solution.py:342
  25.8 55.7 %collective-permute-start.1 = (bf16[4,3584,128]{2,1,0:T(8,128)(2,1)}, bf16[4,3584,128]{2,1,0:T(8,128)(2,1)}, u32[]{:S(2)}, u32[]{:S(2)}) collective-permute-start(bf16[4,3584,128]{2,1,0:T(8,128)(2,1)} %refs_5_.3), channel_id=1, source_target_pairs={{6,0},{25,1},{0,2},{27,3},{2,4},{29,5},{4,6},{31,7},{14,8},{1,9},{... | collective-permute-start | bytes 11010056 | tf_op jit(solution)/shard_map/ppermute | solution.py:342
  54.1 5.2 %collective-permute-start.2 = (bf16[192,3712]{1,0:T(8,128)(2,1)}, bf16[192,3712]{1,0:T(8,128)(2,1)S(1)}, u32[]{:S(2)}, u32[]{:S(2)}) collective-permute-start(bf16[192,3712]{1,0:T(8,128)(2,1)} %get-tuple-element.45), channel_id=1, source_target_pairs={{0,1},{1,0},{2,3},{3,2},{4,5},{5,4},{6,7},{7,6},{8,9},{9,8},{10,11... | collective-permute-start | bytes 4276232 | tf_op jit(solution)/shard_map/ppermute | solution.py:370
  54.2 29.7 %collective-permute-start.3 = (bf16[192,3712]{1,0:T(8,128)(2,1)}, bf16[192,3712]{1,0:T(8,128)(2,1)S(1)}, u32[]{:S(2)}, u32[]{:S(2)}) collective-permute-start(bf16[192,3712]{1,0:T(8,128)(2,1)} %get-tuple-element.50), channel_id=1, source_target_pairs={{0,8},{1,3},{2,10},{3,5},{4,12},{5,7},{6,14},{7,1},{8,16},{9,11},{... | collective-permute-start | bytes 4276232 | tf_op jit(solution)/shard_map/ppermute | solution.py:371
  83.9 27.9 %collective-permute-start.10 = (bf16[192,3712]{1,0:T(8,128)(2,1)}, bf16[192,3712]{1,0:T(8,128)(2,1)S(1)}, u32[]{:S(2)}, u32[]{:S(2)}) collective-permute-start(bf16[192,3712]{1,0:T(8,128)(2,1)} %get-tuple-element.57), channel_id=1, source_target_pairs={{0,16},{1,5},{2,18},{3,7},{4,20},{5,1},{6,22},{7,3},{8,24},{9,13},... | collective-permute-start | bytes 4276232 | tf_op jit(solution)/shard_map/ppermute | solution.py:371
  85.4 59.7 %collective-permute-start.11 = (bf16[192,3712]{1,0:T(8,128)(2,1)}, bf16[192,3712]{1,0:T(8,128)(2,1)S(1)}, u32[]{:S(2)}, u32[]{:S(2)}) collective-permute-start(bf16[192,3712]{1,0:T(8,128)(2,1)} %get-tuple-element.58), channel_id=1, source_target_pairs={{0,24},{1,7},{2,26},{3,1},{4,28},{5,3},{6,30},{7,5},{8,0},{9,15},{... | collective-permute-start | bytes 4276232 | tf_op jit(solution)/shard_map/ppermute | solution.py:371
  88.2 57.2 %collective-permute-start.12 = (bf16[2,3584,128]{2,1,0:T(8,128)(2,1)S(1)}, bf16[2,3584,128]{2,1,0:T(8,128)(2,1)S(1)}, u32[]{:S(2)}, u32[]{:S(2)}) collective-permute-start(bf16[2,3584,128]{2,1,0:T(8,128)(2,1)S(1)} %slice.6), channel_id=1, source_target_pairs={{2,0},{9,1},{4,2},{11,3},{6,4},{13,5},{0,6},{15,7},{10,8},{17,9},{... | collective-permute-start | bytes 5505032 | tf_op jit(solution)/shard_map/ppermute | solution.py:342
  92.6 52.8 %collective-permute-start.13 = (bf16[2,3584,128]{2,1,0:T(8,128)(2,1)S(1)}, bf16[2,3584,128]{2,1,0:T(8,128)(2,1)S(1)}, u32[]{:S(2)}, u32[]{:S(2)}) collective-permute-start(bf16[2,3584,128]{2,1,0:T(8,128)(2,1)S(1)} %slice.7), channel_id=1, source_target_pairs={{6,0},{25,1},{0,2},{27,3},{2,4},{29,5},{4,6},{31,7},{14,8},{1,9},{... | collective-permute-start | bytes 5505032 | tf_op jit(solution)/shard_map/ppermute | solution.py:342
  92.7 72.2 %collective-permute-start.7 = (bf16[192,3712]{1,0:T(8,128)(2,1)}, bf16[192,3712]{1,0:T(8,128)(2,1)S(1)}, u32[]{:S(2)}, u32[]{:S(2)}) collective-permute-start(bf16[192,3712]{1,0:T(8,128)(2,1)} %get-tuple-element.52), channel_id=1, source_target_pairs={{0,3},{1,8},{2,5},{3,10},{4,7},{5,12},{6,1},{7,14},{8,11},{9,16},{... | collective-permute-start | bytes 4276232 | tf_op jit(solution)/shard_map/ppermute | solution.py:378
  111.8 53.2 %collective-permute-start.8 = (bf16[192,3712]{1,0:T(8,128)(2,1)}, bf16[192,3712]{1,0:T(8,128)(2,1)}, u32[]{:S(2)}, u32[]{:S(2)}) collective-permute-start(bf16[192,3712]{1,0:T(8,128)(2,1)} %get-tuple-element.53), channel_id=1, source_target_pairs={{0,5},{1,16},{2,7},{3,18},{4,1},{5,20},{6,3},{7,22},{8,13},{9,24},... | collective-permute-start | bytes 4276232 | tf_op jit(solution)/shard_map/ppermute | solution.py:378
  145.1 28.3 %collective-permute-start.9 = (bf16[192,3712]{1,0:T(8,128)(2,1)}, bf16[192,3712]{1,0:T(8,128)(2,1)}, u32[]{:S(2)}, u32[]{:S(2)}) collective-permute-start(bf16[192,3712]{1,0:T(8,128)(2,1)} %get-tuple-element.54), channel_id=1, source_target_pairs={{0,7},{1,24},{2,1},{3,26},{4,3},{5,28},{6,5},{7,30},{8,15},{9,0},{... | collective-permute-start | bytes 4276232 | tf_op jit(solution)/shard_map/ppermute | solution.py:378
  159.0 26.1 %collective-permute-start.14 = (bf16[192,2304]{1,0:T(8,128)(2,1)}, bf16[192,2304]{1,0:T(8,128)(2,1)S(1)}, u32[]{:S(2)}, u32[]{:S(2)}) collective-permute-start(bf16[192,2304]{1,0:T(8,128)(2,1)} %get-tuple-element.63), channel_id=1, source_target_pairs={{8,0},{3,1},{10,2},{5,3},{12,4},{7,5},{14,6},{1,7},{16,8},{11,9},{... | collective-permute-start | bytes 2654216 | tf_op jit(solution)/shard_map/ppermute | solution.py:382
  164.9 20.2 %collective-permute-start.15 = (bf16[192,2304]{1,0:T(8,128)(2,1)}, bf16[192,2304]{1,0:T(8,128)(2,1)S(1)}, u32[]{:S(2)}, u32[]{:S(2)}) collective-permute-start(bf16[192,2304]{1,0:T(8,128)(2,1)} %get-tuple-element.65), channel_id=1, source_target_pairs={{24,0},{7,1},{26,2},{1,3},{28,4},{3,5},{30,6},{5,7},{0,8},{15,9},{... | collective-permute-start | bytes 2654216 | tf_op jit(solution)/shard_map/ppermute | solution.py:382
  185.2 24.4 %collective-permute-start.16 = (bf16[3584,1152]{1,0:T(8,128)(2,1)}, bf16[3584,1152]{1,0:T(8,128)(2,1)}, u32[]{:S(2)}, u32[]{:S(2)}) collective-permute-start(bf16[3584,1152]{1,0:T(8,128)(2,1)} %all-gather.4.cloned.1.call-done), channel_id=1, source_target_pairs={{0,1},{1,0},{2,3},{3,2},{4,5},{5,4},{6,7},{7,6},{8,9},{9,8},{10,11... | collective-permute-start | bytes 24772616 | tf_op jit(solution)/shard_map/ppermute | solution.py:386
  186.0 39.5 %collective-permute-start.17 = (bf16[192,2304]{1,0:T(8,128)(2,1)S(1)}, bf16[192,2304]{1,0:T(8,128)(2,1)S(1)}, u32[]{:S(2)}, u32[]{:S(2)}) collective-permute-start(bf16[192,2304]{1,0:T(8,128)(2,1)S(1)} %copy-done.15), channel_id=1, source_target_pairs={{16,0},{5,1},{18,2},{7,3},{20,4},{1,5},{22,6},{3,7},{24,8},{13,9},... | collective-permute-start | bytes 2654216 | tf_op jit(solution)/shard_map/ppermute | solution.py:382
  189.5 36.1 %collective-permute-start.18 = (bf16[192,2304]{1,0:T(8,128)(2,1)}, bf16[192,2304]{1,0:T(8,128)(2,1)S(1)}, u32[]{:S(2)}, u32[]{:S(2)}) collective-permute-start(bf16[192,2304]{1,0:T(8,128)(2,1)} %get-tuple-element.78), channel_id=1, source_target_pairs={{1,0},{0,1},{3,2},{2,3},{5,4},{4,5},{7,6},{6,7},{9,8},{8,9},{11,10... | collective-permute-start | bytes 2654216 | tf_op jit(solution)/shard_map/ppermute | solution.py:385
  190.3 35.3 %collective-permute-start.19 = (bf16[192,2304]{1,0:T(8,128)(2,1)}, bf16[192,2304]{1,0:T(8,128)(2,1)S(1)}, u32[]{:S(2)}, u32[]{:S(2)}) collective-permute-start(bf16[192,2304]{1,0:T(8,128)(2,1)} %get-tuple-element.79), channel_id=1, source_target_pairs={{3,0},{8,1},{5,2},{10,3},{7,4},{12,5},{1,6},{14,7},{11,8},{16,9},{... | collective-permute-start | bytes 2654216 | tf_op jit(solution)/shard_map/ppermute | solution.py:385
  192.0 33.5 %collective-permute-start.20 = (bf16[192,2304]{1,0:T(8,128)(2,1)}, bf16[192,2304]{1,0:T(8,128)(2,1)S(1)}, u32[]{:S(2)}, u32[]{:S(2)}) collective-permute-start(bf16[192,2304]{1,0:T(8,128)(2,1)} %get-tuple-element.80), channel_id=1, source_target_pairs={{5,0},{16,1},{7,2},{18,3},{1,4},{20,5},{3,6},{22,7},{13,8},{24,9},... | collective-permute-start | bytes 2654216 | tf_op jit(solution)/shard_map/ppermute | solution.py:385
  209.6 16.0 %collective-permute-start.21 = (bf16[192,2304]{1,0:T(8,128)(2,1)S(1)}, bf16[192,2304]{1,0:T(8,128)(2,1)S(1)}, u32[]{:S(2)}, u32[]{:S(2)}) collective-permute-start(bf16[192,2304]{1,0:T(8,128)(2,1)S(1)} %copy-done.16), channel_id=1, source_target_pairs={{7,0},{24,1},{1,2},{26,3},{3,4},{28,5},{5,6},{30,7},{15,8},{0,9},{... | collective-permute-start | bytes 2654216 | tf_op jit(solution)/shard_map/ppermute | solution.py:385
  (19 other events, 242.5 us)
Sparse Core Ops, SparseCore 0:
  25.2 42.5 all-gather.5
  84.0 82.7 all-gather.3
